TPU v7x, 128 devices: a whole 4x4x4 slice. The times are simulated.
128 devices in a mesh: lat: 8 (over z, x_hi), lon: 16 (over x_lo, y, core).
Axes of the slice: x: 4 (x_hi: 2, x_lo: 2; x = x_hi * 2 + x_lo), y: 4, z: 4, core: 2. Of those that a mesh axis runs over, the one named last changes fastest.
Arguments:
- obs_values: bfloat16 [128, 128, 8, 128], P(('lat', 'lon')), may hold values from -6 to 6
- obs_cells: int32 [128, 128, 8], P(('lat', 'lon')), may hold values from 0 to 767
- obs_counts: int32 [128, 128], P(('lat', 'lon')), may hold values from 1 to 8, as said below
- embed_weight: bfloat16 [128, 256], replicated, may hold values from -0.5 to 0.5
- density_row: float32 [256], replicated, may hold values from -6 to 6
- conv_weight: bfloat16 [2, 3, 3, 256, 256], replicated, may hold values from -0.125 to 0.125
- grid_cotangent: bfloat16 [128, 768, 256], P('lat', 'lon'), may hold values from -6 to 6
Outputs:
- grid_out: bfloat16 [128, 768, 256], P('lat', 'lon')
- grad_conv: float32 [2, 3, 3, 256, 256], replicated
- grad_embed: float32 [128, 256], replicated
- grad_obs: bfloat16 [128, 128, 8, 128], P(('lat', 'lon'))
Inputs may be any that keep to these rules, and one draw needn't show every extreme that they name: `obs_counts`: in every draw one destination tile receives all 8 slots used from every sender; the loads of the other tiles differ from tile to tile.
All inputs are finite; a program needn't handle non-finite values.
Results may differ from a plain program's by a relative error of at most 0.0085.
Values may be sent and summed in bfloat16 or wider, within the bound.
A program may use at most 64 MiB of HBM per device.

v0:
```python
import jax
import jax.numpy as jnp
from jax import lax
from jax.sharding import PartitionSpec as P


def padded_2(cells, sides, width, closed):
    for axis, dim in sides:
        count = lax.axis_size(axis)
        ends = count if closed else count - 1
        head = lax.slice_in_dim(cells, 0, width, axis=dim)
        tail = lax.slice_in_dim(cells, cells.shape[dim] - width, cells.shape[dim], axis=dim)
        cells = jnp.concatenate(
            [
                lax.ppermute(tail, axis, [(i, (i + 1) % count) for i in range(ends)]),
                cells,
                lax.ppermute(head, axis, [((i + 1) % count, i) for i in range(ends)]),
            ],
            axis=dim,
        )
    return cells


def gelu_grad(pre_act, upstream):
    return jax.vjp(jax.nn.gelu, pre_act)[1](upstream)[0]


def pad_rims(field):
    padded = padded_2(field, (("lon", 1),), 1, True)
    return padded_2(padded, (("lat", 0),), 1, False)


def conv_forward(padded, weight, row_count, col_count):
    summed = jnp.zeros((row_count * col_count, weight.shape[-1]), jnp.float32)
    for tap_row in range(3):
        for tap_col in range(3):
            window = padded[tap_row : tap_row + row_count, tap_col : tap_col + col_count].reshape(
                row_count * col_count, -1
            )
            summed = summed + jnp.dot(
                window, weight[tap_row, tap_col], preferred_element_type=jnp.float32
            )
    return summed


def conv_backward(padded_grad, weight, row_count, col_count):
    summed = jnp.zeros((row_count * col_count, weight.shape[-2]), jnp.float32)
    for tap_row in range(3):
        for tap_col in range(3):
            window = padded_grad[
                2 - tap_row : 2 - tap_row + row_count, 2 - tap_col : 2 - tap_col + col_count
            ].reshape(row_count * col_count, -1)
            summed = summed + lax.dot_general(
                window,
                weight[tap_row, tap_col],
                (((1,), (1,)), ((), ())),
                preferred_element_type=jnp.float32,
            )
    return summed


def kernel_grad(padded, pre_grad, row_count, col_count):
    taps = []
    for tap_row in range(3):
        for tap_col in range(3):
            window = padded[tap_row : tap_row + row_count, tap_col : tap_col + col_count].reshape(
                row_count * col_count, -1
            )
            taps.append(
                lax.dot_general(
                    window, pre_grad, (((0,), (0,)), ((), ())), preferred_element_type=jnp.float32
                )
            )
    return jnp.stack(taps).reshape(3, 3, pre_grad.shape[1], pre_grad.shape[1])


def body(obs_values, obs_cells, obs_counts, embed_weight, density_row, conv_weight, grid_cotangent):
    lat_count = lax.axis_size("lat")
    lon_count = lax.axis_size("lon")
    tiles = lat_count * lon_count
    slots = obs_cells.shape[2]
    width = obs_values.shape[3]
    row_count, col_count, chans = grid_cotangent.shape
    depth = conv_weight.shape[0]
    cell_count = row_count * col_count
    send_vals = obs_values[0]
    send_cells = obs_cells[0]
    send_counts = obs_counts[0]
    got_vals, got_cells, got_counts = (
        lax.all_to_all(send_vals, ("lat", "lon"), split_axis=0, concat_axis=0, tiled=True),
        lax.all_to_all(send_cells, ("lat", "lon"), split_axis=0, concat_axis=0, tiled=True),
        lax.all_to_all(send_counts, ("lat", "lon"), split_axis=0, concat_axis=0, tiled=True),
    )
    flat_vals = got_vals.reshape(-1, width)
    slot_valid = (jnp.arange(slots, dtype=jnp.int32)[None, :] < got_counts[:, None]).reshape(-1)
    codes = jnp.where(slot_valid, got_cells.reshape(-1), -1)
    all_rows = codes.shape[0]
    block = min(512, all_rows)
    cell_ids = jnp.arange(cell_count, dtype=jnp.int32)
    code_blocks = codes.reshape(-1, block)

    def accumulate(carry, item):
        sums, numbers = carry
        vals_block, codes_block = item
        onehot = (cell_ids[:, None] == codes_block[None, :]).astype(jnp.bfloat16)
        sums = sums + jnp.dot(onehot, vals_block, preferred_element_type=jnp.float32)
        numbers = numbers + jnp.sum(onehot, axis=1, dtype=jnp.float32)
        return ((sums, numbers), None)

    start_carry = (
        jnp.zeros((cell_count, width), jnp.float32),
        jnp.zeros((cell_count,), jnp.float32),
    )
    (sums, numbers), unused = lax.scan(
        accumulate, start_carry, (flat_vals.reshape(-1, block, width), code_blocks)
    )
    divisor = jnp.maximum(numbers, 1.0)
    cell_means = (sums / divisor[:, None]).astype(jnp.bfloat16)
    embedded = (
        jnp.dot(cell_means, embed_weight, preferred_element_type=jnp.float32)
        + jnp.log1p(numbers)[:, None] * density_row[None, :]
    )
    field = embedded.astype(jnp.bfloat16).reshape(row_count, col_count, chans)
    stored_pads = []
    stored_pre = []
    for layer_idx in range(depth):
        padded = pad_rims(field)
        pre_act = conv_forward(padded, conv_weight[layer_idx], row_count, col_count)
        stored_pads.append(padded)
        stored_pre.append(pre_act)
        field = (
            (field.reshape(-1, chans).astype(jnp.float32) + jax.nn.gelu(pre_act))
            .astype(jnp.bfloat16)
            .reshape(row_count, col_count, chans)
        )
    upstream = grid_cotangent.reshape(-1, chans).astype(jnp.float32)
    kernel_grads = [None] * depth
    for layer_idx in reversed(range(depth)):
        pre_grad = gelu_grad(stored_pre[layer_idx], upstream).astype(jnp.bfloat16)
        local_kernel = kernel_grad(stored_pads[layer_idx], pre_grad, row_count, col_count)
        kernel_grads[layer_idx] = local_kernel
        padded_grad = pad_rims(pre_grad.reshape(row_count, col_count, chans))
        upstream = upstream + conv_backward(
            padded_grad, conv_weight[layer_idx], row_count, col_count
        )
    top_grad = upstream.astype(jnp.bfloat16)
    local_embed = lax.dot_general(
        cell_means, top_grad, (((0,), (0,)), ((), ())), preferred_element_type=jnp.float32
    )
    grad_conv, grad_embed = lax.psum((jnp.stack(kernel_grads), local_embed), ("lat", "lon"))
    mean_grad = lax.dot_general(
        top_grad, embed_weight, (((1,), (1,)), ((), ())), preferred_element_type=jnp.float32
    )
    scaled = (mean_grad / divisor[:, None]).astype(jnp.bfloat16)

    def spread(carry, codes_block):
        onehot = (cell_ids[:, None] == codes_block[None, :]).astype(jnp.bfloat16)
        picked = lax.dot_general(
            onehot, scaled, (((0,), (0,)), ((), ())), preferred_element_type=jnp.float32
        )
        return (carry, picked.astype(jnp.bfloat16))

    unused_carry, picked_all = lax.scan(spread, jnp.zeros((), jnp.int32), code_blocks)
    back_rows = picked_all.reshape(tiles, slots, width)
    returned = lax.all_to_all(back_rows, ("lat", "lon"), split_axis=0, concat_axis=0, tiled=True)
    grad_obs = returned.reshape(1, tiles, slots, width)
    return (field, grad_conv, grad_embed, grad_obs)


def solution(mesh):
    return jax.shard_map(
        body,
        mesh=mesh,
        in_specs=(
            P(("lat", "lon"), None, None, None),
            P(("lat", "lon"), None, None),
            P(("lat", "lon"), None),
            P(),
            P(),
            P(),
            P("lat", "lon", None),
        ),
        out_specs=(P("lat", "lon", None), P(), P(), P(("lat", "lon"), None, None, None)),
        check_vma=False,
    )
```

profile of v0, /device:TPU:1, one launch (start us, length us, event | category | flops | bytes accessed | tf_op | source)
XLA Modules:
  0.0 316.1 jit_solution(10315162191004472304)
XLA Ops:
  7.2 1.4 copy.17
  8.6 11.5 %all-to-all-start = ((s32[128,1,1]{2,1,0:T(1,128)}), s32[128,1,1]{2,1,0:T(1,128)S(1)}, u32[]{:S(2)}, u32[]{:S(2)}) async-start(s32[128,1,1]{2,1,0:T(1,128)} %copy.17), calls=%async_computation | async-start | bytes 131072 | tf_op jit(solution)/shard_map/all_to_all | solution.py:92
  20.9 8.7 %all-to-all-done = s32[128,1,1]{2,1,0:T(1,128)S(1)} async-done(((s32[128,1,1]{2,1,0:T(1,128)}), s32[128,1,1]{2,1,0:T(1,128)S(1)}, u32[]{:S(2)}, u32[]{:S(2)}) %all-to-all-start) | async-done | bytes 544 | tf_op jit(solution)/shard_map/all_to_all | solution.py:92
  29.6 13.8 %all_to_all.28 = s32[128,1,8]{2,1,0:T(1,128)S(1)} all-to-all(s32[128,1,8]{2,1,0:T(1,128)S(1)} %bitcast.368), channel_id=1, replica_groups=mesh['lat'=8,'lon'=16] {'lat','lon'}, dimensions={0} | all-to-all | bytes 8192 | tf_op jit(solution)/shard_map/all_to_all | solution.py:91
  43.4 4.4 %all-to-all-start.2 = ((bf16[128,8,128]{2,1,0:T(8,128)(2,1)}), bf16[128,8,128]{2,1,0:T(8,128)(2,1)S(1)}, u32[]{:S(2)}, u32[]{:S(2)}) async-start(bf16[128,8,128]{2,1,0:T(8,128)(2,1)} %bitcast.365), calls=%async_computation.2 | async-start | bytes 524288 | tf_op jit(solution)/shard_map/all_to_all | solution.py:90
  47.9 1.8 slice_bitcast_fusion
  49.8 2.4 reduce
  53.0 0.8 reduce.4
  53.9 5.0 %all-to-all-done.2 = bf16[128,8,128]{2,1,0:T(8,128)(2,1)S(1)} async-done(((bf16[128,8,128]{2,1,0:T(8,128)(2,1)}), bf16[128,8,128]{2,1,0:T(8,128)(2,1)S(1)}, u32[]{:S(2)}, u32[]{:S(2)}) %all-to-all-start.2) | async-done | bytes 262176 | tf_op jit(solution)/shard_map/all_to_all | solution.py:90
  58.9 1.4 while.25
  62.4 2.3 collective-permute-done.1
  64.8 3.0 collective-permute-start.2
  67.8 1.3 collective-permute-start.3
  69.4 4.6 %collective-permute-done.3 = bf16[1,50,256]{2,1,0:T(8,128)(2,1)S(1)} collective-permute-done((bf16[1,50,256]{2,1,0:T(8,128)(2,1)S(1)}, bf16[1,50,256]{2,1,0:T(8,128)(2,1)S(1)}, u32[]{:S(2)}, u32[]{:S(2)}) %collective-permute-start.3) | collective-permute-done | bytes 25632 | tf_op jit(solution)/shard_map/ppermute | solution.py:17
  77.4 1.4 collective-permute-start.4
  78.8 1.9 collective-permute-start.5
  82.0 4.8 %collective-permute-start.6 = (bf16[1,50,256]{2,1,0:T(8,128)(2,1)S(1)}, bf16[1,50,256]{2,1,0:T(8,128)(2,1)S(1)}, u32[]{:S(2)}, u32[]{:S(2)}) collective-permute-start(bf16[1,50,256]{2,1,0:T(8,128)(2,1)S(1)} %get-tuple-element.155), channel_id=1, source_target_pairs={{0,16},{16,32},{32,48},{48,64},{64,80},{80,96},{96,112},{1,17},{17... | collective-permute-start | bytes 76808 | tf_op jit(solution)/shard_map/ppermute | solution.py:15
  86.8 1.5 collective-permute-start.7
  88.6 4.6 %collective-permute-done.7 = bf16[1,50,256]{2,1,0:T(8,128)(2,1)S(1)} collective-permute-done((bf16[1,50,256]{2,1,0:T(8,128)(2,1)S(1)}, bf16[1,50,256]{2,1,0:T(8,128)(2,1)S(1)}, u32[]{:S(2)}, u32[]{:S(2)}) %collective-permute-start.7) | collective-permute-done | bytes 25632 | tf_op jit(solution)/shard_map/ppermute | solution.py:17
  96.6 1.6 fusion.60
  99.5 5.1 %collective-permute-start.9 = (bf16[16,1,256]{2,1,0:T(2,128)(2,1)S(1)}, bf16[16,1,256]{2,1,0:T(2,128)(2,1)S(1)}, u32[]{:S(2)}, u32[]{:S(2)}) collective-permute-start(bf16[16,1,256]{2,1,0:T(2,128)(2,1)S(1)} %get-tuple-element.168), channel_id=1, source_target_pairs={{1,0},{2,1},{3,2},{4,3},{5,4},{6,5},{7,6},{8,7},{9,8},{10,9},{11,1... | collective-permute-start | bytes 24584 | tf_op jit(solution)/shard_map/ppermute | solution.py:17
  107.2 1.3 collective-permute-start.10
  108.5 5.5 %collective-permute-start.11 = (bf16[1,50,256]{2,1,0:T(8,128)(2,1)S(1)}, bf16[1,50,256]{2,1,0:T(8,128)(2,1)S(1)}, u32[]{:S(2)}, u32[]{:S(2)}) collective-permute-start(bf16[1,50,256]{2,1,0:T(8,128)(2,1)S(1)} %get-tuple-element.152), channel_id=1, source_target_pairs={{0,16},{16,32},{32,48},{48,64},{64,80},{80,96},{96,112},{1,17},{17... | collective-permute-start | bytes 76808 | tf_op jit(solution)/shard_map/ppermute | solution.py:15
  119.3 5.2 %collective-permute-start.13 = (bf16[16,1,256]{2,1,0:T(2,128)(2,1)S(1)}, bf16[16,1,256]{2,1,0:T(2,128)(2,1)S(1)}, u32[]{:S(2)}, u32[]{:S(2)}) collective-permute-start(bf16[16,1,256]{2,1,0:T(2,128)(2,1)S(1)} %get-tuple-element.164), channel_id=1, source_target_pairs={{1,0},{2,1},{3,2},{4,3},{5,4},{6,5},{7,6},{8,7},{9,8},{10,9},{11,1... | collective-permute-start | bytes 24584 | tf_op jit(solution)/shard_map/ppermute | solution.py:17
  127.1 2.6 pad_maximum_fusion
  129.7 1.3 collective-permute-start.14
  131.0 6.0 %collective-permute-start.15 = (bf16[1,50,256]{2,1,0:T(8,128)(2,1)S(1)}, bf16[1,50,256]{2,1,0:T(8,128)(2,1)S(1)}, u32[]{:S(2)}, u32[]{:S(2)}) collective-permute-start(bf16[1,50,256]{2,1,0:T(8,128)(2,1)S(1)} %get-tuple-element.148), channel_id=1, source_target_pairs={{0,16},{16,32},{32,48},{48,64},{64,80},{80,96},{96,112},{1,17},{17... | collective-permute-start | bytes 76808 | tf_op jit(solution)/shard_map/ppermute | solution.py:15
  141.1 1.0 fusion.76
  142.5 1.4 while.24
  143.9 23.6 %all_to_all.29 = bf16[128,8,128]{2,1,0:T(8,128)(2,1)S(1)} all-to-all(bf16[128,8,128]{2,1,0:T(8,128)(2,1)S(1)} %bitcast.367), channel_id=1, replica_groups=mesh['lat'=8,'lon'=16] {'lat','lon'}, dimensions={0} | all-to-all | bytes 524288 | tf_op jit(solution)/shard_map/all_to_all | solution.py:165
  167.4 135.5 %all-reduce.3.cloned.1.call-done = (f32[2,3,3,256,256]{4,3,2,1,0:T(8,128)}, f32[128,256]{1,0:T(8,128)}) async-done(((f32[2,3,3,256,256]{4,3,2,1,0:T(8,128)}, f32[128,256]{1,0:T(8,128)}), (f32[2,3,3,256,256]{4,3,2,1,0:T(8,128)}, f32[128,256]{1,0:T(8,128)})) %all-reduce.3.cloned.1.call-update) | async-done | bytes 4849680 | tf_op jit(solution)/shard_map/psum | solution.py:150
  303.0 5.0 %copy.56 = f32[2,3,3,256,256]{4,3,2,1,0:T(8,128)} copy(f32[2,3,3,256,256]{4,3,2,1,0:T(8,128)} %get-tuple-element.283) | data formatting | bytes 9437184
  (132 shorter events, 32.3 us)
Async XLA Ops:
  7.2 53.2 %copy-start = (bf16[128,256]{1,0:T(8,128)(2,1)S(1)}, bf16[128,256]{1,0:T(8,128)(2,1)}, u32[]{:S(2)}) copy-start(bf16[128,256]{1,0:T(8,128)(2,1)} %param.14) | copy-start | bytes 196612
  8.6 21.0 %all-to-all-start = ((s32[128,1,1]{2,1,0:T(1,128)}), s32[128,1,1]{2,1,0:T(1,128)S(1)}, u32[]{:S(2)}, u32[]{:S(2)}) async-start(s32[128,1,1]{2,1,0:T(1,128)} %copy.17), calls=%async_computation | async-start | bytes 131072 | tf_op jit(solution)/shard_map/all_to_all | solution.py:92
  43.4 15.5 %all-to-all-start.2 = ((bf16[128,8,128]{2,1,0:T(8,128)(2,1)}), bf16[128,8,128]{2,1,0:T(8,128)(2,1)S(1)}, u32[]{:S(2)}, u32[]{:S(2)}) async-start(bf16[128,8,128]{2,1,0:T(8,128)(2,1)} %bitcast.365), calls=%async_computation.2 | async-start | bytes 524288 | tf_op jit(solution)/shard_map/all_to_all | solution.py:90
  47.8 255.1 %all-reduce.3.cloned.1.call-start = ((), (), s32[]{:S(2)}) async-start(), calls=%async_computation.4 | async-start | bytes 9699328 | tf_op jit(solution)/shard_map/psum | solution.py:150
  58.9 1.5 copy-start.3
  60.8 1.6 collective-permute-start
  61.6 3.2 %collective-permute-start.1 = (bf16[16,1,256]{2,1,0:T(2,128)(2,1)S(1)}, bf16[16,1,256]{2,1,0:T(2,128)(2,1)S(1)}, u32[]{:S(2)}, u32[]{:S(2)}) collective-permute-start(bf16[16,1,256]{2,1,0:T(2,128)(2,1)S(1)} %get-tuple-element.176), channel_id=1, source_target_pairs={{1,0},{2,1},{3,2},{4,3},{5,4},{6,5},{7,6},{8,7},{9,8},{10,9},{11,1... | collective-permute-start | bytes 24584 | tf_op jit(solution)/shard_map/ppermute | solution.py:17
  64.8 4.6 %collective-permute-start.2 = (bf16[1,50,256]{2,1,0:T(8,128)(2,1)S(1)}, bf16[1,50,256]{2,1,0:T(8,128)(2,1)S(1)}, u32[]{:S(2)}, u32[]{:S(2)}) collective-permute-start(bf16[1,50,256]{2,1,0:T(8,128)(2,1)S(1)} %get-tuple-element.159), channel_id=1, source_target_pairs={{0,16},{16,32},{32,48},{48,64},{64,80},{80,96},{96,112},{1,17},{17... | collective-permute-start | bytes 76808 | tf_op jit(solution)/shard_map/ppermute | solution.py:15
  67.8 6.3 %collective-permute-start.3 = (bf16[1,50,256]{2,1,0:T(8,128)(2,1)S(1)}, bf16[1,50,256]{2,1,0:T(8,128)(2,1)S(1)}, u32[]{:S(2)}, u32[]{:S(2)}) collective-permute-start(bf16[1,50,256]{2,1,0:T(8,128)(2,1)S(1)} %get-tuple-element.160), channel_id=1, source_target_pairs={{16,0},{32,16},{48,32},{64,48},{80,64},{96,80},{112,96},{17,1},{33... | collective-permute-start | bytes 76808 | tf_op jit(solution)/shard_map/ppermute | solution.py:17
  77.4 3.9 %collective-permute-start.4 = (bf16[16,1,256]{2,1,0:T(2,128)(2,1)S(1)}, bf16[16,1,256]{2,1,0:T(2,128)(2,1)S(1)}, u32[]{:S(2)}, u32[]{:S(2)}) collective-permute-start(bf16[16,1,256]{2,1,0:T(2,128)(2,1)S(1)} %get-tuple-element.171), channel_id=1, source_target_pairs={{0,1},{1,2},{2,3},{3,4},{4,5},{5,6},{6,7},{7,8},{8,9},{9,10},{10,1... | collective-permute-start | bytes 24584 | tf_op jit(solution)/shard_map/ppermute | solution.py:15
  78.8 3.2 %collective-permute-start.5 = (bf16[16,1,256]{2,1,0:T(2,128)(2,1)S(1)}, bf16[16,1,256]{2,1,0:T(2,128)(2,1)S(1)}, u32[]{:S(2)}, u32[]{:S(2)}) collective-permute-start(bf16[16,1,256]{2,1,0:T(2,128)(2,1)S(1)} %get-tuple-element.172), channel_id=1, source_target_pairs={{1,0},{2,1},{3,2},{4,3},{5,4},{6,5},{7,6},{8,7},{9,8},{10,9},{11,1... | collective-permute-start | bytes 24584 | tf_op jit(solution)/shard_map/ppermute | solution.py:17
  82.0 6.6 %collective-permute-start.6 = (bf16[1,50,256]{2,1,0:T(8,128)(2,1)S(1)}, bf16[1,50,256]{2,1,0:T(8,128)(2,1)S(1)}, u32[]{:S(2)}, u32[]{:S(2)}) collective-permute-start(bf16[1,50,256]{2,1,0:T(8,128)(2,1)S(1)} %get-tuple-element.155), channel_id=1, source_target_pairs={{0,16},{16,32},{32,48},{48,64},{64,80},{80,96},{96,112},{1,17},{17... | collective-permute-start | bytes 76808 | tf_op jit(solution)/shard_map/ppermute | solution.py:15
  86.8 6.3 %collective-permute-start.7 = (bf16[1,50,256]{2,1,0:T(8,128)(2,1)S(1)}, bf16[1,50,256]{2,1,0:T(8,128)(2,1)S(1)}, u32[]{:S(2)}, u32[]{:S(2)}) collective-permute-start(bf16[1,50,256]{2,1,0:T(8,128)(2,1)S(1)} %get-tuple-element.156), channel_id=1, source_target_pairs={{16,0},{32,16},{48,32},{64,48},{80,64},{96,80},{112,96},{17,1},{33... | collective-permute-start | bytes 76808 | tf_op jit(solution)/shard_map/ppermute | solution.py:17
  95.6 1.0 copy-start.2
  98.8 8.3 %collective-permute-start.8 = (bf16[16,1,256]{2,1,0:T(2,128)(2,1)S(1)}, bf16[16,1,256]{2,1,0:T(2,128)(2,1)S(1)}, u32[]{:S(2)}, u32[]{:S(2)}) collective-permute-start(bf16[16,1,256]{2,1,0:T(2,128)(2,1)S(1)} %get-tuple-element.167), channel_id=1, source_target_pairs={{0,1},{1,2},{2,3},{3,4},{4,5},{5,6},{6,7},{7,8},{8,9},{9,10},{10,1... | collective-permute-start | bytes 24584 | tf_op jit(solution)/shard_map/ppermute | solution.py:15
  99.5 7.6 %collective-permute-start.9 = (bf16[16,1,256]{2,1,0:T(2,128)(2,1)S(1)}, bf16[16,1,256]{2,1,0:T(2,128)(2,1)S(1)}, u32[]{:S(2)}, u32[]{:S(2)}) collective-permute-start(bf16[16,1,256]{2,1,0:T(2,128)(2,1)S(1)} %get-tuple-element.168), channel_id=1, source_target_pairs={{1,0},{2,1},{3,2},{4,3},{5,4},{6,5},{7,6},{8,7},{9,8},{10,9},{11,1... | collective-permute-start | bytes 24584 | tf_op jit(solution)/shard_map/ppermute | solution.py:17
  107.2 7.1 %collective-permute-start.10 = (bf16[1,50,256]{2,1,0:T(8,128)(2,1)S(1)}, bf16[1,50,256]{2,1,0:T(8,128)(2,1)S(1)}, u32[]{:S(2)}, u32[]{:S(2)}) collective-permute-start(bf16[1,50,256]{2,1,0:T(8,128)(2,1)S(1)} %get-tuple-element.151), channel_id=1, source_target_pairs={{16,0},{32,16},{48,32},{64,48},{80,64},{96,80},{112,96},{17,1},{33... | collective-permute-start | bytes 76808 | tf_op jit(solution)/shard_map/ppermute | solution.py:17
  108.5 6.5 %collective-permute-start.11 = (bf16[1,50,256]{2,1,0:T(8,128)(2,1)S(1)}, bf16[1,50,256]{2,1,0:T(8,128)(2,1)S(1)}, u32[]{:S(2)}, u32[]{:S(2)}) collective-permute-start(bf16[1,50,256]{2,1,0:T(8,128)(2,1)S(1)} %get-tuple-element.152), channel_id=1, source_target_pairs={{0,16},{16,32},{32,48},{48,64},{64,80},{80,96},{96,112},{1,17},{17... | collective-permute-start | bytes 76808 | tf_op jit(solution)/shard_map/ppermute | solution.py:15
  119.2 10.5 %collective-permute-start.12 = (bf16[16,1,256]{2,1,0:T(2,128)(2,1)S(1)}, bf16[16,1,256]{2,1,0:T(2,128)(2,1)S(1)}, u32[]{:S(2)}, u32[]{:S(2)}) collective-permute-start(bf16[16,1,256]{2,1,0:T(2,128)(2,1)S(1)} %get-tuple-element.163), channel_id=1, source_target_pairs={{0,1},{1,2},{2,3},{3,4},{4,5},{5,6},{6,7},{7,8},{8,9},{9,10},{10,1... | collective-permute-start | bytes 24584 | tf_op jit(solution)/shard_map/ppermute | solution.py:15
  119.3 10.4 %collective-permute-start.13 = (bf16[16,1,256]{2,1,0:T(2,128)(2,1)S(1)}, bf16[16,1,256]{2,1,0:T(2,128)(2,1)S(1)}, u32[]{:S(2)}, u32[]{:S(2)}) collective-permute-start(bf16[16,1,256]{2,1,0:T(2,128)(2,1)S(1)} %get-tuple-element.164), channel_id=1, source_target_pairs={{1,0},{2,1},{3,2},{4,3},{5,4},{6,5},{7,6},{8,7},{9,8},{10,9},{11,1... | collective-permute-start | bytes 24584 | tf_op jit(solution)/shard_map/ppermute | solution.py:17
  129.7 7.6 %collective-permute-start.14 = (bf16[1,50,256]{2,1,0:T(8,128)(2,1)S(1)}, bf16[1,50,256]{2,1,0:T(8,128)(2,1)S(1)}, u32[]{:S(2)}, u32[]{:S(2)}) collective-permute-start(bf16[1,50,256]{2,1,0:T(8,128)(2,1)S(1)} %get-tuple-element.147), channel_id=1, source_target_pairs={{16,0},{32,16},{48,32},{64,48},{80,64},{96,80},{112,96},{17,1},{33... | collective-permute-start | bytes 76808 | tf_op jit(solution)/shard_map/ppermute | solution.py:17
  131.0 7.0 %collective-permute-start.15 = (bf16[1,50,256]{2,1,0:T(8,128)(2,1)S(1)}, bf16[1,50,256]{2,1,0:T(8,128)(2,1)S(1)}, u32[]{:S(2)}, u32[]{:S(2)}) collective-permute-start(bf16[1,50,256]{2,1,0:T(8,128)(2,1)S(1)} %get-tuple-element.148), channel_id=1, source_target_pairs={{0,16},{16,32},{32,48},{48,64},{64,80},{80,96},{96,112},{1,17},{17... | collective-permute-start | bytes 76808 | tf_op jit(solution)/shard_map/ppermute | solution.py:15
  303.0 5.0 %copy-start.1 = (f32[128,256]{1,0:T(8,128)S(1)}, f32[128,256]{1,0:T(8,128)}, u32[]{:S(2)}) copy-start(f32[128,256]{1,0:T(8,128)} %get-tuple-element.284) | copy-start | bytes 393220
Sparse Core Ops, SparseCore 0:
  142.3 160.5 all-reduce.2
where the time goes:
time: 317 us; the launch traced here: 316 us
  waiting for transfers between devices  164 us (52%)
  starting transfers between devices  55.9 us (18%)
  blocking collectives  37.4 us (12%)
  matrix products  21.5 us (7%)
  between operations  14.8 us (5%)
  local copies, waits for them, and re-layouts  14 us (4%)
  other arithmetic  8.77 us (3%)
    psum x1, waiting for transfers between devices, body(): lax.psum((jnp.stack(kernel_grads), local_embed), ('lat', 'lon'))  136 us
    all_to_all x1, blocking collectives, body(): lax.all_to_all(back_rows, ('lat', 'lon'), split_axis=0, concat_axis=0, ti...  23.6 us
    ppermute x8, starting transfers between devices, padded_2(): lax.ppermute(tail, axis, [(i, (i + 1) % count) for i in range(ends)])  22.3 us
    ppermute x8, starting transfers between devices, padded_2(): lax.ppermute(head, axis, [((i + 1) % count, i) for i in range(ends)])  17.6 us
    all_to_all x1, blocking collectives, body(): lax.all_to_all(send_cells, ('lat', 'lon'), split_axis=0, concat_axis=0, t...  13.8 us
    ppermute x8, waiting for transfers between devices, padded_2(): lax.ppermute(head, axis, [((i + 1) % count, i) for i in range(ends)])  12.1 us
    all_to_all x1, starting transfers between devices, body(): lax.all_to_all(send_counts, ('lat', 'lon'), split_axis=0, concat_axis=0,...  11.5 us
    all_to_all x1, waiting for transfers between devices, body(): lax.all_to_all(send_counts, ('lat', 'lon'), split_axis=0, concat_axis=0,...  8.74 us
  transfers between devices with their start and end apart: 19, of which 11 were waited for; matrix products, arithmetic and copies ran while one was open for 6% of the time, Pallas kernels for 0%

commit v1 on v0

v1 whole, which is shorter than its diff:
```python
import functools

import jax
import jax.numpy as jnp
from jax import lax
from jax.experimental import pallas as pl
from jax.experimental.pallas import tpu as pltpu
from jax.sharding import PartitionSpec as P

MESH = pl.DeviceIdType.MESH
NA, NB = 8, 16
NT = NA * NB
TR, TC = 16, 48
CELLS = TR * TC
CH, F, CAP = 256, 128, 8
SLOTS = NT * CAP
HR = 4
HC = 2
SIDE = 8
W = TC + 2 * SIDE
STRIP = 16
UNITS = 592
F32, BF16 = jnp.float32, jnp.bfloat16
GC, GA = 0.7978845608028654, 0.044715


def coords():
    return lax.axis_index("lat"), lax.axis_index("lon")


def tile_dev(t):
    return (t // NB, lax.rem(t, NB))


def barrier_all():
    a, b = coords()
    me = a * NB + b
    sem = pltpu.get_barrier_semaphore()

    def signal(k, carry):
        t = lax.rem(me + k, NT)
        pl.semaphore_signal(sem, inc=1, device_id=tile_dev(t), device_id_type=MESH)
        return carry

    lax.fori_loop(1, NT, signal, 0)
    pl.semaphore_wait(sem, NT - 1)


def exchange_start(src, dst, send, recv):
    a, b = coords()
    me = a * NB + b

    def go(k, carry):
        t = lax.rem(me + k, NT)
        pltpu.make_async_remote_copy(
            src_ref=src.at[t],
            dst_ref=dst.at[me],
            send_sem=send,
            recv_sem=recv,
            device_id=tile_dev(t),
            device_id_type=MESH,
        ).start()
        return carry

    lax.fori_loop(1, NT, go, 0)
    pltpu.make_async_copy(src.at[me], dst.at[me], recv).start()


def exchange_wait_recv(dst, recv):
    pltpu.make_async_copy(dst, dst, recv).wait()


def exchange_wait_send(src, send):
    part = src.at[pl.ds(0, NT - 1)]
    pltpu.make_async_copy(part, part, send).wait()


DIRS = [(-1, 0), (1, 0), (0, -1), (0, 1), (-1, -1), (-1, 1), (1, -1), (1, 1)]


def halo_copies(src, bufs, rows, send, recv):
    a, b = coords()
    copies = []
    for i, (da, db) in enumerate(DIRS):
        back = DIRS.index((-da, -db))
        row = {-1: pl.ds(0, rows), 0: pl.ds(0, TR), 1: pl.ds(TR - rows, rows)}[da]
        col = {-1: pl.ds(0, STRIP), 0: pl.ds(0, TC), 1: pl.ds(TC - STRIP, STRIP)}[db]
        copies.append(
            pltpu.make_async_remote_copy(
                src_ref=src.at[row, col],
                dst_ref=bufs[back],
                send_sem=send.at[i],
                recv_sem=recv.at[back],
                device_id=(
                    jnp.clip(a + da, 0, NA - 1),
                    lax.rem(b + db + NB, NB),
                ),
                device_id_type=MESH,
            )
        )
    return copies


def when_exists(da, fn):
    a, _ = coords()
    if da == 0:
        fn()
    elif da < 0:
        pl.when(a > 0)(fn)
    else:
        pl.when(a < NA - 1)(fn)


def halo_start(copies):
    for (da, _), copy in zip(DIRS, copies):
        when_exists(da, copy.start)


def halo_wait(src, bufs, rows, send, recv):
    copies = halo_copies(src, bufs, rows, send, recv)
    for i, (da, db) in enumerate(DIRS):
        when_exists(da, copies[i].wait_send)
        back = DIRS.index((-da, -db))
        when_exists(da, copies[back].wait_recv)


def halo_zero(bufs):
    for i, (da, _) in enumerate(DIRS):
        if da:

            def clear(buf=bufs[i]):
                buf[...] = jnp.zeros(buf.shape, buf.dtype)

            a, _ = coords()
            pl.when(a == (0 if da < 0 else NA - 1))(clear)


def ext_row(core, bufs, rows, r):
    if r < rows:
        left, mid, right, k = bufs[4], bufs[0], bufs[5], r
    elif r < rows + TR:
        left, mid, right, k = bufs[2], core, bufs[3], r - rows
    else:
        left, mid, right, k = bufs[6], bufs[1], bufs[7], r - rows - TR
    return jnp.concatenate(
        [
            left[k].astype(F32)[STRIP - SIDE :],
            mid[k].astype(F32),
            right[k].astype(F32)[:SIDE],
        ],
        axis=0,
    )


def put3(dst, rows, value):
    n = value.shape[0] // W
    for q, shift in ((0, 1), (1, 0), (2, value.shape[0] - 1)):
        moved = value if shift == 0 else pltpu.roll(value, shift, 0)
        dst[rows, :, q * CH : (q + 1) * CH] = moved.astype(BF16).reshape(n, W, CH)


def row_mask(first, n):
    rows = lax.broadcasted_iota(jnp.int32, (n * W, CH), 0) // W + first
    return (rows >= 0) & (rows < NA * TR)


def gelu_parts(x):
    x2 = x * x
    t = jnp.tanh(GC * x * (1.0 + GA * x2))
    half = 0.5 * (1.0 + t)
    value = x * half
    slope = half + 0.5 * x * (1.0 - t * t) * (GC * (1.0 + 3.0 * GA * x2))
    return value, slope


def conv_fwd(src, weight, layer, start, n):
    acc = None
    for p in range(3):
        window = src[pl.ds(start + p, n)].reshape(n * W, 3 * CH)
        part = jnp.dot(window, weight[layer, p], preferred_element_type=F32)
        acc = part if acc is None else acc + part
    return acc


def conv_bwd(src, weight, layer, start, n):
    acc = None
    for p in range(3):
        for q in range(3):
            lanes = slice((2 - q) * CH, (3 - q) * CH)
            window = src[pl.ds(start + 2 - p, n), :, lanes].reshape(n * W, CH)
            part = lax.dot_general(
                window,
                weight[layer, p, q * CH : (q + 1) * CH],
                (((1,), (1,)), ((), ())),
                preferred_element_type=F32,
            )
            acc = part if acc is None else acc + part
    return acc


def store_units(dst, first, value):
    n = value.shape[0] // 8
    for h in range(2):
        dst[first : first + n, h] = value[:, h * 128 : (h + 1) * 128].astype(BF16).reshape(n, 8, 128)


def kernel_grad(src, first, grad, dst, unit):
    col = lax.broadcasted_iota(jnp.int32, (TR * W, CH), 0) & (W - 1)
    masked = jnp.where((col >= SIDE) & (col < SIDE + TC), grad.astype(F32), 0.0).astype(BF16)
    for p in range(3):
        window = src[first + p : first + p + TR].reshape(TR * W, 3 * CH)
        taps = lax.dot_general(
            window, masked, (((0,), (0,)), ((), ())), preferred_element_type=F32
        )
        store_units(dst, unit + p * 96, taps)


def main_kernel(
    payload, embed, density, weight, cot,
    out_ref, grads_ref, picked_ref,
    recv, onehot, means, inv, field,
    fN, fS, fW, fE, fNW, fNE, fSW, fSE,
    cN, cS, cW, cE, cNW, cNE, cSW, cSE,
    x0, x1, g1, g0, slope0, cot_ext, up1, grid2, top,
    a2a_sem, halo_send, halo_recv, cot_send, cot_recv,
):
    a, _ = coords()
    fbufs = (fN, fS, fW, fE, fNW, fNE, fSW, fSE)
    cbufs = (cN, cS, cW, cE, cNW, cNE, cSW, cSE)
    barrier_all()
    exchange_start(payload, recv, a2a_sem.at[0], a2a_sem.at[1])
    halo_start(halo_copies(cot, cbufs, HC, cot_send, cot_recv))
    halo_zero(fbufs)
    halo_zero(cbufs)
    halo_wait(cot, cbufs, HC, cot_send, cot_recv)
    for r in range(TR + 2 * HC):
        cot_ext[r] = ext_row(cot, cbufs, HC, r)
    exchange_wait_recv(recv, a2a_sem.at[1])

    group = 16

    def build(i, carry):
        codes = recv[pl.ds(i * group, group), 8:16, :].astype(F32).reshape(group * CAP, F)
        cell = (codes[:, 0:1] * TC + codes[:, 64:65]).astype(jnp.int32)
        lane = lax.broadcasted_iota(jnp.int32, (group * CAP, CELLS), 1)
        onehot[pl.ds(i * group * CAP, group * CAP), :] = jnp.where(cell == lane, 1.0, 0.0).astype(BF16)
        return carry

    lax.fori_loop(0, NT // group, build, 0)
    values = recv[:, 0:8, :].reshape(SLOTS, F)
    both = jnp.concatenate([values, jnp.ones((SLOTS, F), BF16)], axis=1)
    sums = lax.dot_general(
        onehot[...], both, (((0,), (0,)), ((), ())), preferred_element_type=F32
    )
    numbers = sums[:, F:]
    divisor = jnp.maximum(numbers, 1.0)
    inv[...] = divisor
    cell_means = (sums[:, :F] / divisor).astype(BF16)
    means[...] = cell_means
    logs = jnp.log(1.0 + numbers)
    embedded = jnp.dot(cell_means, embed[...], preferred_element_type=F32) + jnp.concatenate(
        [logs, logs], axis=1
    ) * density[...]
    field[...] = embedded.astype(BF16).reshape(TR, TC, CH)

    halo_start(halo_copies(field, fbufs, HR, halo_send, halo_recv))
    halo_wait(field, fbufs, HR, halo_send, halo_recv)
    for r in range(TR + 2 * HR):
        put3(x0, slice(r, r + 1), ext_row(field, fbufs, HR, r))

    n = 11

    def fwd0(c, carry):
        pre = conv_fwd(x0, weight, 0, c * n, n)
        value, slope = gelu_parts(pre)
        old = x0[pl.ds(c * n + 1, n), :, CH : 2 * CH].reshape(n * W, CH).astype(F32)
        new = jnp.where(row_mask(a * TR - 3 + c * n, n), old + value, 0.0)
        new = new.astype(BF16).astype(F32)
        put3(x1, pl.ds(c * n, n), new)
        slope0[pl.ds(c * n, n)] = slope.reshape(n, W, CH)
        return carry

    lax.fori_loop(0, 2, fwd0, 0)
    m = 10

    def fwd1(c, carry):
        pre = conv_fwd(x1, weight, 1, c * m, m)
        value, slope = gelu_parts(pre)
        old = x1[pl.ds(c * m + 1, m), :, CH : 2 * CH].reshape(m * W, CH).astype(F32)
        grid2[pl.ds(c * m, m)] = (old + value).astype(BF16).reshape(m, W, CH)
        grad = cot_ext[pl.ds(c * m, m)].reshape(m * W, CH) * slope
        put3(g1, pl.ds(c * m, m), grad.astype(BF16).astype(F32))
        return carry

    lax.fori_loop(0, 2, fwd1, 0)
    out_ref[...] = grid2[2 : 2 + TR, SIDE : SIDE + TC, :]

    kernel_grad(x1, 2, g1[2 : 2 + TR, :, CH : 2 * CH].reshape(TR * W, CH), grads_ref, 288)
    k = 9

    def bwd1(c, carry):
        up = conv_bwd(g1, weight, 1, c * k, k) + cot_ext[pl.ds(c * k + 1, k)].reshape(k * W, CH)
        up1[pl.ds(c * k, k)] = up.reshape(k, W, CH)
        grad = up * slope0[pl.ds(c * k + 2, k)].reshape(k * W, CH)
        grad = jnp.where(row_mask(a * TR - 1 + c * k, k), grad, 0.0)
        put3(g0, pl.ds(c * k, k), grad.astype(BF16).astype(F32))
        return carry

    lax.fori_loop(0, 2, bwd1, 0)
    kernel_grad(x0, 3, g0[1 : 1 + TR, :, CH : 2 * CH].reshape(TR * W, CH), grads_ref, 0)
    j = 8

    def bwd0(c, carry):
        up = conv_bwd(g0, weight, 0, c * j, j) + up1[pl.ds(c * j + 1, j)].reshape(j * W, CH)
        top[pl.ds(c * j, j)] = up.reshape(j, W, CH)[:, SIDE : SIDE + TC].astype(BF16)
        return carry

    lax.fori_loop(0, 2, bwd0, 0)
    top_grad = top[...].reshape(CELLS, CH)
    store_units(
        grads_ref,
        576,
        lax.dot_general(
            means[...], top_grad, (((0,), (0,)), ((), ())), preferred_element_type=F32
        ),
    )
    mean_grad = lax.dot_general(
        top_grad, embed[...], (((1,), (1,)), ((), ())), preferred_element_type=F32
    )
    scaled = (mean_grad / inv[...]).astype(BF16)
    picked = jnp.dot(onehot[...], scaled, preferred_element_type=F32)
    picked_ref[...] = picked.astype(BF16).reshape(NT, CAP, F)
    exchange_wait_send(payload, a2a_sem.at[0])


ORDERS = (("x", "y", "z"), ("y", "z", "x"), ("z", "x", "y"))


def place():
    a, b = coords()
    return {"z": a // 2, "x": lax.rem(a, 2) * 2 + b // 8, "y": lax.rem(b // 2, 4), "c": lax.rem(b, 2)}


def device_at(pos):
    x = pos["x"]
    return (pos["z"] * 2 + x // 2, lax.rem(x, 2) * 8 + pos["y"] * 2 + pos["c"])


def along(pos, axis, step):
    moved = dict(pos)
    moved[axis] = lax.rem(pos[axis] + step, 4)
    return moved


def remote(src, dst, send, recv, pos):
    copy = pltpu.make_async_remote_copy(
        src_ref=src, dst_ref=dst, send_sem=send, recv_sem=recv,
        device_id=device_at(pos), device_id_type=MESH,
    )
    copy.start()


def wait_bytes(ref, sem):
    pltpu.make_async_copy(ref, ref, sem).wait()


def add_parts(own, got):
    total = own.astype(F32)
    for i in range(3):
        total = total + got[i].astype(F32)
    return total.astype(BF16)


def reduce_kernel(
    grads, picked, total, back,
    pair, own, r1, r2, r3, t1, t2, e1, e2, e3, f1, f2,
    a2a_sem, pair_sem, ssem, rsem, gssem, grsem,
):
    pos = place()
    c = pos["c"]
    sibling = dict(pos)
    sibling["c"] = 1 - c
    barrier_all()
    remote(grads.at[:, 1 - c], pair, pair_sem.at[0], pair_sem.at[1], sibling)
    wait_bytes(pair, pair_sem.at[1])
    own[...] = (grads[:, c].astype(F32) + pair[...].astype(F32)).astype(BF16)

    sizes = (48, 12, 3)
    for s, order in enumerate(ORDERS):
        for step in range(1, 4):
            peer = along(pos, order[0], step)
            first = s * 192 + peer[order[0]] * 48
            remote(own.at[pl.ds(first, 48)], r1.at[s, step - 1], ssem.at[0, s], rsem.at[0, s], peer)
    for step in range(1, 4):
        peer = along(pos, "x", step)
        remote(own.at[pl.ds(576 + peer["x"] * 4, 4)], e1.at[step - 1], ssem.at[0, 3], rsem.at[0, 3], peer)
    exchange_start(picked, back, a2a_sem.at[0], a2a_sem.at[1])
    for s, order in enumerate(ORDERS):
        wait_bytes(r1.at[s], rsem.at[0, s])
        t1[s] = add_parts(own[pl.ds(s * 192 + pos[order[0]] * 48, 48)], r1.at[s])
        for step in range(1, 4):
            peer = along(pos, order[1], step)
            first = peer[order[1]] * 12
            remote(t1.at[s, pl.ds(first, 12)], r2.at[s, step - 1], ssem.at[1, s], rsem.at[1, s], peer)
    wait_bytes(e1, rsem.at[0, 3])
    f1[...] = add_parts(own[pl.ds(576 + pos["x"] * 4, 4)], e1)
    for step in range(1, 4):
        peer = along(pos, "y", step)
        remote(f1.at[pl.ds(peer["y"], 1)], e2.at[step - 1], ssem.at[1, 3], rsem.at[1, 3], peer)
    for s, order in enumerate(ORDERS):
        wait_bytes(r2.at[s], rsem.at[1, s])
        t2[s] = add_parts(t1[s, pl.ds(pos[order[1]] * 12, 12)], r2.at[s])
        for step in range(1, 4):
            peer = along(pos, order[2], step)
            first = peer[order[2]] * 3
            remote(t2.at[s, pl.ds(first, 3)], r3.at[s, step - 1], ssem.at[2, s], rsem.at[2, s], peer)
    wait_bytes(e2, rsem.at[1, 3])
    f2[...] = add_parts(f1[pl.ds(pos["y"], 1)], e2)
    for step in range(1, 4):
        peer = along(pos, "z", step)
        remote(f2, e3.at[step - 1], ssem.at[2, 3], rsem.at[2, 3], peer)

    base = [s * 192 + pos[o[0]] * 48 + pos[o[1]] * 12 + pos[o[2]] * 3 for s, o in enumerate(ORDERS)]
    for s, order in enumerate(ORDERS):
        wait_bytes(r3.at[s], rsem.at[2, s])
        total[pl.ds(base[s], 3), c] = add_parts(t2[s, pl.ds(pos[order[2]] * 3, 3)], r3.at[s])
        block = total.at[pl.ds(base[s], 3), c]
        for step in range(1, 4):
            remote(block, block, gssem.at[0, s], grsem.at[0, s], along(pos, order[2], step))
    wait_bytes(e3, rsem.at[2, 3])
    ebase = 576 + pos["x"] * 4 + pos["y"]
    total[pl.ds(ebase, 1), c] = add_parts(f2[...], e3)
    block = total.at[pl.ds(ebase, 1), c]
    for step in range(1, 4):
        remote(block, block, gssem.at[0, 3], grsem.at[0, 3], along(pos, "y", step))
    for s, order in enumerate(ORDERS):
        wait_bytes(total.at[pl.ds(0, 9), c], grsem.at[0, s])
        block = total.at[pl.ds(s * 192 + pos[order[0]] * 48 + pos[order[1]] * 12, 12), c]
        for step in range(1, 4):
            remote(block, block, gssem.at[1, s], grsem.at[1, s], along(pos, order[1], step))
    wait_bytes(total.at[pl.ds(0, 3), c], grsem.at[0, 3])
    block = total.at[pl.ds(576 + pos["x"] * 4, 4), c]
    for step in range(1, 4):
        remote(block, block, gssem.at[1, 3], grsem.at[1, 3], along(pos, "x", step))
    for s, order in enumerate(ORDERS):
        wait_bytes(total.at[pl.ds(0, 36), c], grsem.at[1, s])
        block = total.at[pl.ds(s * 192 + pos[order[0]] * 48, 48), c]
        for step in range(1, 4):
            remote(block, block, gssem.at[2, s], grsem.at[2, s], along(pos, order[0], step))
    wait_bytes(total.at[pl.ds(0, 12), c], grsem.at[1, 3])
    for s in range(3):
        wait_bytes(total.at[pl.ds(0, 144), c], grsem.at[2, s])
    half = total.at[:, c]
    remote(half, half, pair_sem.at[2], pair_sem.at[3], sibling)

    exchange_wait_recv(back, a2a_sem.at[1])
    exchange_wait_send(picked, a2a_sem.at[0])
    wait_bytes(pair, pair_sem.at[0])
    for phase in range(3):
        for s in range(3):
            wait_bytes(own.at[pl.ds(0, 3 * sizes[phase])], ssem.at[phase, s])
            wait_bytes(own.at[pl.ds(0, 3 * sizes[2 - phase])], gssem.at[phase, s])
    for phase, units in enumerate((12, 3, 3)):
        wait_bytes(own.at[pl.ds(0, units)], ssem.at[phase, 3])
    for phase, units in enumerate((3, 12)):
        wait_bytes(own.at[pl.ds(0, units)], gssem.at[phase, 3])
    wait_bytes(pair, pair_sem.at[2])
    wait_bytes(pair, pair_sem.at[3])


VM = pl.BlockSpec(memory_space=pltpu.VMEM)
DMA = pltpu.SemaphoreType.DMA


def vmem(shape, dtype=BF16):
    return pltpu.VMEM(shape, dtype)


def halo_shapes(rows):
    wide, side, corner = (rows, TC, CH), (TR, STRIP, CH), (rows, STRIP, CH)
    return [vmem(s) for s in (wide, wide, side, side, corner, corner, corner, corner)]


def body(obs_values, obs_cells, obs_counts, embed_weight, density_row, conv_weight, grid_cotangent):
    cells, counts = obs_cells[0], obs_counts[0]
    used = jnp.arange(CAP, dtype=jnp.int32)[None, :] < counts[:, None]
    row = jnp.where(used, cells // TC, -100)[:, :, None]
    col = (cells % TC)[:, :, None]
    lane = jnp.arange(F, dtype=jnp.int32)[None, None, :]
    codes = jnp.where(lane < 64, row, col).astype(BF16)
    payload = jnp.concatenate([obs_values[0], codes], axis=1)
    weight = conv_weight.reshape(2, 3, 3 * CH, CH)
    field, grads, picked = pl.pallas_call(
        main_kernel,
        out_shape=[
            jax.ShapeDtypeStruct((TR, TC, CH), BF16),
            jax.ShapeDtypeStruct((UNITS, 2, 8, 128), BF16),
            jax.ShapeDtypeStruct((NT, CAP, F), BF16),
        ],
        in_specs=[VM] * 5,
        out_specs=[VM] * 3,
        scratch_shapes=[
            vmem((NT, 16, F)), vmem((SLOTS, CELLS)), vmem((CELLS, F)), vmem((CELLS, F), F32),
            vmem((TR, TC, CH)), *halo_shapes(HR), *halo_shapes(HC),
            vmem((24, W, 3 * CH)), vmem((22, W, 3 * CH)), vmem((20, W, 3 * CH)), vmem((18, W, 3 * CH)),
            vmem((22, W, CH), F32), vmem((20, W, CH), F32), vmem((18, W, CH), F32),
            vmem((20, W, CH)), vmem((TR, TC, CH)),
            DMA((2,)), DMA((8,)), DMA((8,)), DMA((8,)), DMA((8,)),
        ],
        compiler_params=pltpu.CompilerParams(
            collective_id=0, has_side_effects=True, vmem_limit_bytes=56 * 2**20
        ),
    )(payload, embed_weight, density_row.reshape(1, CH), weight, grid_cotangent)
    total, back = pl.pallas_call(
        reduce_kernel,
        out_shape=[
            jax.ShapeDtypeStruct((UNITS, 2, 8, 128), BF16),
            jax.ShapeDtypeStruct((NT, CAP, F), BF16),
        ],
        in_specs=[VM] * 2,
        out_specs=[VM] * 2,
        scratch_shapes=[
            vmem((UNITS, 8, 128)), vmem((UNITS, 8, 128)),
            vmem((3, 3, 48, 8, 128)), vmem((3, 3, 12, 8, 128)), vmem((3, 3, 3, 8, 128)),
            vmem((3, 48, 8, 128)), vmem((3, 12, 8, 128)),
            vmem((3, 4, 8, 128)), vmem((3, 1, 8, 128)), vmem((3, 1, 8, 128)),
            vmem((4, 8, 128)), vmem((1, 8, 128)),
            DMA((2,)), DMA((4,)), DMA((3, 4)), DMA((3, 4)), DMA((3, 4)), DMA((3, 4)),
        ],
        compiler_params=pltpu.CompilerParams(
            collective_id=1, has_side_effects=True, vmem_limit_bytes=40 * 2**20
        ),
    )(grads, picked)
    whole = total.transpose(0, 2, 1, 3).reshape(UNITS * 8, CH).astype(F32)
    grad_conv = whole[:4608].reshape(2, 3, 3, CH, CH)
    return field, grad_conv, whole[4608:], back[None]


def solution(mesh):
    return jax.shard_map(
        body,
        mesh=mesh,
        in_specs=(
            P(("lat", "lon"), None, None, None),
            P(("lat", "lon"), None, None),
            P(("lat", "lon"), None),
            P(),
            P(),
            P(),
            P("lat", "lon", None),
        ),
        out_specs=(P("lat", "lon", None), P(), P(), P(("lat", "lon"), None, None, None)),
        check_vma=False,
    )
```

time: 317 us -> 108 us (0.34)
  waiting for transfers between devices: 164 us -> 0 us
  Pallas kernels: 0 us -> 96.5 us
  starting transfers between devices: 55.9 us -> 0 us
  blocking collectives: 37.4 us -> 0 us
  matrix products: 21.5 us -> 0 us
  between operations: 14.8 us -> 0.68 us
  local copies, waits for them, and re-layouts: 14 us -> 7.44 us
  other arithmetic: 8.77 us -> 3.26 us
    psum x1 -> x0, waiting for transfers between devices: 136 us -> none  [body(): lax.psum((jnp.stack(kernel_grads), local_embed), ('lat', 'lon'))]
    pallas_call x0 -> x2, Pallas kernels: none -> 96.5 us  [the longest x1 53 us: body(): pl.pallas_call(main_kernel, out_shape=[jax.ShapeDtypeStruct((TR, TC, CH),...]
    ppermute x16 -> x0, starting transfers between devices: 40 us -> none  [the longest x8 22.3 us: padded_2(): lax.ppermute(tail, axis, [(i, (i + 1) % count) for i in range(ends)])]
    all_to_all x2 -> x0, blocking collectives: 37.4 us -> none  [the longest x1 23.6 us: body(): lax.all_to_all(back_rows, ('lat', 'lon'), split_axis=0, concat_axis=0, ti...]
    dot_general x61 -> x0, matrix products: 21.5 us -> none  [the longest x18 6.33 us: conv_forward(): jnp.dot(window, weight[tap_row, tap_col], preferred_element_type=jnp.floa...]
    all_to_all x2 -> x0, starting transfers between devices: 15.9 us -> none  [the longest x1 11.5 us: body(): lax.all_to_all(send_counts, ('lat', 'lon'), split_axis=0, concat_axis=0,...]
    ppermute x16 -> x0, waiting for transfers between devices: 14.4 us -> none  [the longest x8 12.1 us: padded_2(): lax.ppermute(head, axis, [((i + 1) % count, i) for i in range(ends)])]
    all_to_all x2 -> x0, waiting for transfers between devices: 13.8 us -> none  [the longest x1 8.74 us: body(): lax.all_to_all(send_counts, ('lat', 'lon'), split_axis=0, concat_axis=0,...]
  transfers between devices with their start and end apart: 19 -> 0, of which waited for: 11 -> 0; matrix products, arithmetic and copies ran while one was open for 6% -> 0% of each run, Pallas kernels for 0% -> 0%
where the time goes in v1:
time: 108 us
  Pallas kernels  96.5 us (89%)
  local copies, waits for them, and re-layouts  7.44 us (7%)
  other arithmetic  3.26 us (3%)
    pallas_call x1, Pallas kernels, body(): pl.pallas_call(main_kernel, out_shape=[jax.ShapeDtypeStruct((TR, TC, CH),...  53 us
    pallas_call x1, Pallas kernels, body(): pl.pallas_call(reduce_kernel, out_shape=[jax.ShapeDtypeStruct((UNITS, 2,...  43.5 us
    unnamed x8, local copies, waits for them, and re-layouts  4.08 us
    slice x1, local copies, waits for them, and re-layouts, body(): grad_conv = whole[:4608].reshape(2, 3, 3, CH, CH)  2.49 us

profile of v1, /device:TPU:1, one launch (start us, length us, event | category | flops | bytes accessed | tf_op | source)
XLA Modules:
  0.0 107.9 jit_solution(11507134886529747520)
XLA Ops:
  0.6 0.7 fusion
  1.3 0.1 copy.11
  1.5 0.1 copy.12
  1.6 0.3 select_convert_fusion
  1.9 1.8 %pad_maximum_fusion.payload = bf16[128,16,128]{2,1,0:T(8,128)(2,1)} fusion(bf16[128,8,128]{2,1,0:T(8,128)(2,1)S(1)} %select_convert_fusion, bf16[128,8,128]{2,1,0:T(8,128)(2,1)} %bitcast.33), kind=kLoop, calls=%fused_computation.1 | loop fusion | flops 1048576 | bytes 1048576 | tf_op jit(solution)/shard_map/concatenate | solution.py:491
  3.7 53.0 %shard_map.102 = (bf16[16,48,256]{2,1,0:T(8,128)(2,1)}, bf16[592,2,8,128]{3,2,1,0:T(8,128)(2,1)}, bf16[128,8,128]{2,1,0:T(8,128)(2,1)}) custom-call(bf16[128,16,128]{2,1,0:T(8,128)(2,1)} %pad_maximum_fusion.payload, bf16[128,256]{1,0:T(8,128)(2,1)} %embed.1, f32[1,256]{1,0:T(1,128)} %bitcast.34, bf16[2,3,768,256]{3,2,1,0:T(8,128)(2,1)} %bitcast.32, ...), custom_call_target="tpu_custom_call" | custom-call | tf_op jit(solution)/shard_map/pallas_call | solution.py:493
  56.8 0.0 copy-start
  56.8 1.7 %copy-done = bf16[592,2,8,128]{3,2,1,0:T(8,128)(2,1)S(1)} copy-done((bf16[592,2,8,128]{3,2,1,0:T(8,128)(2,1)S(1)}, bf16[592,2,8,128]{3,2,1,0:T(8,128)(2,1)}, u32[]{:S(2)}) %copy-start) | copy-done | bytes 2424856
  58.5 0.0 copy-start.1
  58.5 0.9 copy-done.1
  59.4 43.5 %shard_map.103 = (bf16[592,2,8,128]{3,2,1,0:T(8,128)(2,1)S(1)}, bf16[128,8,128]{2,1,0:T(8,128)(2,1)S(1)}) custom-call(bf16[592,2,8,128]{3,2,1,0:T(8,128)(2,1)S(1)} %copy-done, bf16[128,8,128]{2,1,0:T(8,128)(2,1)S(1)} %copy-done.1), custom_call_target="tpu_custom_call" | custom-call | tf_op jit(solution)/shard_map/pallas_call | solution.py:514
  102.9 0.4 convert_bitcast_fusion
  103.3 0.7 slice_bitcast_fusion
  103.9 0.0 copy-start.2
  103.9 2.5 %slice.13 = f32[576,8,2,128]{3,1,2,0:T(8,128)} slice(f32[592,8,2,128]{3,1,2,0:T(8,128)S(1)} %convert_bitcast_fusion), slice={[0:576], [0:8], [0:2], [0:128]} | slice | bytes 9437184 | tf_op jit(solution)/shard_map/slice | solution.py:535
  106.4 0.0 copy-done.2
  106.4 0.7 copy.15
  107.2 0.7 copy.16
  (1 shorter events, 0.0 us)
Async XLA Ops:
  56.8 1.7 %copy-start = (bf16[592,2,8,128]{3,2,1,0:T(8,128)(2,1)S(1)}, bf16[592,2,8,128]{3,2,1,0:T(8,128)(2,1)}, u32[]{:S(2)}) copy-start(bf16[592,2,8,128]{3,2,1,0:T(8,128)(2,1)} %get-tuple-element.10.grads) | copy-start | bytes 7274500
  58.5 0.9 copy-start.1
  103.9 2.5 %copy-start.2 = (bf16[16,48,256]{2,1,0:T(8,128)(2,1)S(1)}, bf16[16,48,256]{2,1,0:T(8,128)(2,1)}, u32[]{:S(2)}) copy-start(bf16[16,48,256]{2,1,0:T(8,128)(2,1)} %get-tuple-element.20) | copy-start | bytes 1179652

commit v2 on v1

v2 whole, which is shorter than its diff:
```python
import functools

import jax
import jax.numpy as jnp
from jax import lax
from jax.experimental import pallas as pl
from jax.experimental.pallas import tpu as pltpu
from jax.sharding import PartitionSpec as P

MESH = pl.DeviceIdType.MESH
NA, NB = 8, 16
NT = NA * NB
TR, TC = 16, 48
CELLS = TR * TC
CH, F, CAP = 256, 128, 8
SLOTS = NT * CAP
HR = 4
HC = 2
SIDE = 8
W = TC + 2 * SIDE
STRIP = 16
UNITS = 592
F32, BF16 = jnp.float32, jnp.bfloat16
GC, GA = 0.7978845608028654, 0.044715


def coords():
    return lax.axis_index("lat"), lax.axis_index("lon")


def tile_dev(t):
    return (t // NB, lax.rem(t, NB))


def barrier_signal():
    a, b = coords()
    me = a * NB + b
    sem = pltpu.get_barrier_semaphore()

    def signal(k, carry):
        t = lax.rem(me + k, NT)
        pl.semaphore_signal(sem, inc=1, device_id=tile_dev(t), device_id_type=MESH)
        return carry

    lax.fori_loop(1, NT, signal, 0)


def barrier_wait():
    pl.semaphore_wait(pltpu.get_barrier_semaphore(), NT - 1)


def exchange_start(src, dst, send, recv):
    a, b = coords()
    me = a * NB + b

    def go(k, carry):
        ta = lax.rem(a + k // NB, NA)
        tb = lax.rem(b + lax.rem(k, NB), NB)
        pltpu.make_async_remote_copy(
            src_ref=src.at[ta * NB + tb],
            dst_ref=dst.at[me],
            send_sem=send,
            recv_sem=recv.at[a],
            device_id=(ta, tb),
            device_id_type=MESH,
        ).start()
        return carry

    pltpu.make_async_copy(src.at[me], dst.at[me], recv.at[a]).start()
    lax.fori_loop(1, NT, go, 0)


def exchange_wait_recv(dst, recv, lat):
    part = dst.at[pl.ds(lat * NB, NB)]
    pltpu.make_async_copy(part, part, recv.at[lat]).wait()


def exchange_wait_send(src, send):
    part = src.at[pl.ds(0, NT - 1)]
    pltpu.make_async_copy(part, part, send).wait()


DIRS = [(-1, 0), (1, 0), (0, -1), (0, 1), (-1, -1), (-1, 1), (1, -1), (1, 1)]


def halo_copies(src, bufs, rows, send, recv):
    a, b = coords()
    copies = []
    for i, (da, db) in enumerate(DIRS):
        back = DIRS.index((-da, -db))
        row = {-1: pl.ds(0, rows), 0: pl.ds(0, TR), 1: pl.ds(TR - rows, rows)}[da]
        col = {-1: pl.ds(0, STRIP), 0: pl.ds(0, TC), 1: pl.ds(TC - STRIP, STRIP)}[db]
        copies.append(
            pltpu.make_async_remote_copy(
                src_ref=src.at[row, col],
                dst_ref=bufs[back],
                send_sem=send.at[i],
                recv_sem=recv.at[back],
                device_id=(
                    jnp.clip(a + da, 0, NA - 1),
                    lax.rem(b + db + NB, NB),
                ),
                device_id_type=MESH,
            )
        )
    return copies


def when_exists(da, fn):
    a, _ = coords()
    if da == 0:
        fn()
    elif da < 0:
        pl.when(a > 0)(fn)
    else:
        pl.when(a < NA - 1)(fn)


def halo_start(copies):
    for (da, _), copy in zip(DIRS, copies):
        when_exists(da, copy.start)


def halo_wait(src, bufs, rows, send, recv):
    copies = halo_copies(src, bufs, rows, send, recv)
    for i, (da, db) in enumerate(DIRS):
        when_exists(da, copies[i].wait_send)
        back = DIRS.index((-da, -db))
        when_exists(da, copies[back].wait_recv)


def halo_zero(bufs):
    for i, (da, _) in enumerate(DIRS):
        if da:

            def clear(buf=bufs[i]):
                buf[...] = jnp.zeros(buf.shape, buf.dtype)

            a, _ = coords()
            pl.when(a == (0 if da < 0 else NA - 1))(clear)


def ext_row(core, bufs, rows, r):
    if r < rows:
        left, mid, right, k = bufs[4], bufs[0], bufs[5], r
    elif r < rows + TR:
        left, mid, right, k = bufs[2], core, bufs[3], r - rows
    else:
        left, mid, right, k = bufs[6], bufs[1], bufs[7], r - rows - TR
    return jnp.concatenate(
        [
            left[k].astype(F32)[STRIP - SIDE :],
            mid[k].astype(F32),
            right[k].astype(F32)[:SIDE],
        ],
        axis=0,
    )


def put3(dst, rows, value):
    n = value.shape[0] // W
    for q, shift in ((0, 1), (1, 0), (2, value.shape[0] - 1)):
        moved = value if shift == 0 else pltpu.roll(value, shift, 0)
        dst[rows, :, q * CH : (q + 1) * CH] = moved.astype(BF16).reshape(n, W, CH)


def row_mask(first, n):
    rows = lax.broadcasted_iota(jnp.int32, (n * W, CH), 0) // W + first
    return (rows >= 0) & (rows < NA * TR)


def gelu_parts(x):
    x2 = x * x
    t = jnp.tanh(GC * x * (1.0 + GA * x2))
    half = 0.5 * (1.0 + t)
    value = x * half
    slope = half + 0.5 * x * (1.0 - t * t) * (GC * (1.0 + 3.0 * GA * x2))
    return value, slope


def conv_fwd(src, weight, layer, start, n):
    acc = None
    for p in range(3):
        window = src[pl.ds(start + p, n)].reshape(n * W, 3 * CH)
        part = jnp.dot(window, weight[layer, p], preferred_element_type=F32)
        acc = part if acc is None else acc + part
    return acc


def conv_bwd(src, weight, layer, start, n):
    acc = None
    for p in range(3):
        for q in range(3):
            lanes = slice((2 - q) * CH, (3 - q) * CH)
            window = src[pl.ds(start + 2 - p, n), :, lanes].reshape(n * W, CH)
            part = lax.dot_general(
                window,
                weight[layer, p, q * CH : (q + 1) * CH],
                (((1,), (1,)), ((), ())),
                preferred_element_type=F32,
            )
            acc = part if acc is None else acc + part
    return acc


def store_units(dst, first, value):
    n = value.shape[0] // 8
    for h in range(2):
        dst[first : first + n, h] = value[:, h * 128 : (h + 1) * 128].astype(BF16).reshape(n, 8, 128)


def kernel_grad(src, first, grad, dst, unit, taps_of):
    col = lax.broadcasted_iota(jnp.int32, (TR * W, CH), 0) & (W - 1)
    masked = jnp.where((col >= SIDE) & (col < SIDE + TC), grad.astype(F32), 0.0).astype(BF16)
    for p in taps_of:
        window = src[first + p : first + p + TR].reshape(TR * W, 3 * CH)
        taps = lax.dot_general(
            window, masked, (((0,), (0,)), ((), ())), preferred_element_type=F32
        )
        store_units(dst, unit + p * 96, taps)


ORDERS = (("x", "y", "z"), ("y", "z", "x"), ("z", "x", "y"))
WAVES = ((384, 1), (0, 2))
EMBED0, EMBED_UNITS = 576, 16


def place():
    a, b = coords()
    return {"z": a // 2, "x": lax.rem(a, 2) * 2 + b // 8, "y": lax.rem(b // 2, 4), "c": lax.rem(b, 2)}


def device_at(pos):
    x = pos["x"]
    return (pos["z"] * 2 + x // 2, lax.rem(x, 2) * 8 + pos["y"] * 2 + pos["c"])


def along(pos, axis, step):
    moved = dict(pos)
    moved[axis] = lax.rem(pos[axis] + step, 4)
    return moved


def other_core(pos):
    moved = dict(pos)
    moved["c"] = 1 - pos["c"]
    return moved


def remote(src, dst, send, recv, pos):
    pltpu.make_async_remote_copy(
        src_ref=src, dst_ref=dst, send_sem=send, recv_sem=recv,
        device_id=device_at(pos), device_id_type=MESH,
    ).start()


def wait_bytes(ref, sem):
    pltpu.make_async_copy(ref, ref, sem).wait()


def add_parts(own, got, count):
    total = own.astype(F32)
    for i in range(count):
        total = total + got[i].astype(F32)
    return total.astype(BF16)


def on_plane(pos, axes, fn):
    def step(k, carry):
        peer = along(along(pos, axes[0], k // 4), axes[1], lax.rem(k, 4))
        fn(peer, k - 1)
        return carry

    lax.fori_loop(1, 16, step, 0)


class Wave:
    def __init__(self, w, pos, grads, total, bufs, sems):
        self.first, self.per = WAVES[w]
        self.pos, self.grads, self.total = pos, grads, total
        self.pair, self.own, self.r1, self.t1, self.r2 = bufs
        self.pair_sem, self.sem = sems
        self.stream = 64 * self.per

    def send(self, s, phase):
        return self.sem.at[s, phase, 0]

    def recv(self, s, phase):
        return self.sem.at[s, phase, 1]

    def mine(self):
        return self.grads.at[pl.ds(self.first, 3 * self.stream), 1 - self.pos["c"]]

    def pair_start(self):
        remote(self.mine(), self.pair, self.pair_sem.at[0], self.pair_sem.at[1], other_core(self.pos))

    def rs1_start(self):
        pos, part = self.pos, 16 * self.per
        wait_bytes(self.pair, self.pair_sem.at[1])
        kept = self.grads[pl.ds(self.first, 3 * self.stream), pos["c"]]
        self.own[...] = (kept.astype(F32) + self.pair[...].astype(F32)).astype(BF16)
        for step in (2, 1, 3):
            for s, order in enumerate(ORDERS):
                peer = along(pos, order[0], step)
                src = self.own.at[pl.ds(s * self.stream + peer[order[0]] * part, part)]
                remote(src, self.r1.at[s, step - 1], self.send(s, 0), self.recv(s, 0), peer)

    def rs2_start(self):
        pos, part, per = self.pos, 16 * self.per, self.per
        for s, order in enumerate(ORDERS):
            wait_bytes(self.r1.at[s], self.recv(s, 0))
            kept = self.own[pl.ds(s * self.stream + pos[order[0]] * part, part)]
            self.t1[s] = add_parts(kept, self.r1.at[s], 3)

            def go(peer, k, s=s, order=order):
                src = self.t1.at[s, pl.ds((peer[order[1]] * 4 + peer[order[2]]) * per, per)]
                remote(src, self.r2.at[s, k], self.send(s, 1), self.recv(s, 1), peer)

            on_plane(pos, order[1:], go)

    def block(self, s, order):
        pos, per = self.pos, self.per
        start = self.first + s * self.stream + pos[order[0]] * 16 * per
        return start, (pos[order[1]] * 4 + pos[order[2]]) * per

    def ag2_start(self):
        pos, per, c = self.pos, self.per, self.pos["c"]
        for s, order in enumerate(ORDERS):
            wait_bytes(self.r2.at[s], self.recv(s, 1))
            start, inner = self.block(s, order)
            self.total[pl.ds(start + inner, per), c] = add_parts(
                self.t1[s, pl.ds(inner, per)], self.r2.at[s], 15
            )
            block = self.total.at[pl.ds(start + inner, per), c]

            def go(peer, k, s=s, block=block):
                remote(block, block, self.send(s, 2), self.recv(s, 2), peer)

            on_plane(pos, order[1:], go)

    def ag1_start(self):
        pos, per, c = self.pos, self.per, self.pos["c"]
        for s, order in enumerate(ORDERS):
            wait_bytes(self.total.at[pl.ds(0, 15 * per), c], self.recv(s, 2))
            start, _ = self.block(s, order)
            block = self.total.at[pl.ds(start, 16 * per), c]
            for step in (2, 1, 3):
                remote(block, block, self.send(s, 3), self.recv(s, 3), along(pos, order[0], step))

    def pair2_start(self):
        c = self.pos["c"]
        for s in range(3):
            wait_bytes(self.total.at[pl.ds(0, 48 * self.per), c], self.recv(s, 3))
            block = self.total.at[pl.ds(self.first + s * self.stream, self.stream), c]
            remote(block, block, self.send(s, 4), self.recv(s, 4), other_core(self.pos))

    def finish(self):
        c, per = self.pos["c"], self.per
        wait_bytes(self.pair, self.pair_sem.at[0])
        for s in range(3):
            for phase, units in enumerate((48, 15, 15, 48, 64)):
                wait_bytes(self.total.at[pl.ds(0, units * per), c], self.send(s, phase))
            wait_bytes(self.total.at[pl.ds(0, self.stream), c], self.recv(s, 4))


class EmbedSum:
    def __init__(self, pos, grads, total, bufs, sem):
        self.pos, self.grads, self.total, self.sem = pos, grads, total, sem
        self.pair, self.own, self.r1, self.t1, self.r2 = bufs

    def pair_start(self):
        src = self.grads.at[pl.ds(EMBED0, EMBED_UNITS), 1 - self.pos["c"]]
        remote(src, self.pair, self.sem.at[0, 0], self.sem.at[0, 1], other_core(self.pos))

    def rs_start(self):
        pos = self.pos
        wait_bytes(self.pair, self.sem.at[0, 1])
        kept = self.grads[pl.ds(EMBED0, EMBED_UNITS), pos["c"]]
        self.own[...] = (kept.astype(F32) + self.pair[...].astype(F32)).astype(BF16)

        def go(peer, k):
            src = self.own.at[pl.ds(peer["y"] * 4 + peer["z"], 1)]
            remote(src, self.r1.at[k], self.sem.at[1, 0], self.sem.at[1, 1], peer)

        on_plane(pos, ("y", "z"), go)

    def sum_start(self):
        pos = self.pos
        wait_bytes(self.r1, self.sem.at[1, 1])
        self.t1[...] = add_parts(self.own[pl.ds(pos["y"] * 4 + pos["z"], 1)], self.r1, 15)
        for step in range(1, 4):
            remote(self.t1, self.r2.at[step - 1], self.sem.at[2, 0], self.sem.at[2, 1], along(pos, "x", step))

    def ag_start(self):
        pos, c = self.pos, self.pos["c"]
        wait_bytes(self.r2, self.sem.at[2, 1])
        at = EMBED0 + pos["y"] * 4 + pos["z"]
        parts = []
        for i in range(4):
            got = self.t1[...].astype(F32)
            for step in range(1, 4):
                got = jnp.where(lax.rem(pos["x"] - step + 4, 4) == i, self.r2[step - 1].astype(F32), got)
            parts.append(got)
        self.total[pl.ds(at, 1), c] = (((parts[0] + parts[1]) + parts[2]) + parts[3]).astype(BF16)
        block = self.total.at[pl.ds(at, 1), c]
        on_plane(
            pos, ("y", "z"),
            lambda peer, k: remote(block, block, self.sem.at[3, 0], self.sem.at[3, 1], peer),
        )

    def pair2_start(self):
        c = self.pos["c"]
        wait_bytes(self.total.at[pl.ds(0, 15), c], self.sem.at[3, 1])
        block = self.total.at[pl.ds(EMBED0, EMBED_UNITS), c]
        remote(block, block, self.sem.at[4, 0], self.sem.at[4, 1], other_core(self.pos))

    def finish(self):
        c = self.pos["c"]
        for phase, units in enumerate((16, 15, 3, 15, 16)):
            wait_bytes(self.total.at[pl.ds(0, units), c], self.sem.at[phase, 0])
        wait_bytes(self.total.at[pl.ds(0, 16), c], self.sem.at[4, 1])


def make_payload(payload, values, cells, counts, table):
    eye = lax.broadcasted_iota(jnp.int32, (NT, NT), 0) == lax.broadcasted_iota(jnp.int32, (NT, NT), 1)
    used = jnp.where(eye, counts[...].astype(F32), 0.0).sum(axis=1, keepdims=True)
    slot = lax.broadcasted_iota(jnp.int32, (NT, CAP), 1).astype(F32)
    cell = cells[...]
    row = (cell * 1366) >> 16
    table[...] = jnp.zeros_like(table)
    table[:, 0:CAP] = jnp.where(slot < used, row.astype(F32), -100.0)
    table[:, CAP : 2 * CAP] = (cell - row * TC).astype(F32)
    spread = jnp.broadcast_to(table[...][:, None, :], (NT, CAP, F)).reshape(SLOTS, F)
    sub = lax.broadcasted_iota(jnp.int32, (SLOTS, F), 0) & (CAP - 1)
    lane = lax.broadcasted_iota(jnp.int32, (SLOTS, F), 1)
    spread = jnp.where((lane & (CAP - 1)) == sub, spread, 0.0).astype(BF16)
    l0 = lax.broadcasted_iota(jnp.int32, (F, F), 0)
    l1 = lax.broadcasted_iota(jnp.int32, (F, F), 1)
    pick = ((l0 < CAP) & (l1 < 64)) | ((l0 >= CAP) & (l0 < 2 * CAP) & (l1 >= 64))
    codes = jnp.dot(spread, jnp.where(pick, 1.0, 0.0).astype(BF16), preferred_element_type=F32)
    payload[:, 0:CAP, :] = values[...]
    payload[:, CAP : 2 * CAP, :] = codes.astype(BF16).reshape(NT, CAP, F)


def kernel(
    values_hbm, cells_hbm, counts_hbm, embed_hbm, density_hbm, weight_hbm, cot_hbm,
    out_ref, total, back,
    values, cells, counts, embed, density, weight, cot, table,
    payload, recv, onehot, means, inv, field,
    fN, fS, fW, fE, fNW, fNE, fSW, fSE,
    cN, cS, cW, cE, cNW, cNE, cSW, cSE,
    x0, x1, g1, g0, slope0, cot_ext, up1, grid2, top, grads, picked,
    *rest,
):
    w1_bufs, w2_bufs, e_bufs = rest[0:5], rest[5:10], rest[10:15]
    (load_sem, a2a_send, a2a_recv, halo_send, halo_recv, cot_send, cot_recv,
     w1_pair, w1_sem, w2_pair, w2_sem, e_sem) = rest[15:]
    a, _ = coords()
    pos = place()
    fbufs = (fN, fS, fW, fE, fNW, fNE, fSW, fSE)
    cbufs = (cN, cS, cW, cE, cNW, cNE, cSW, cSE)
    w1 = Wave(0, pos, grads, total, w1_bufs, (w1_pair, w1_sem))
    w2 = Wave(1, pos, grads, total, w2_bufs, (w2_pair, w2_sem))
    es = EmbedSum(pos, grads, total, e_bufs, e_sem)
    loads = [
        pltpu.make_async_copy(src, dst, load_sem.at[i])
        for i, (src, dst) in enumerate(
            (
                (cells_hbm, cells), (counts_hbm, counts), (values_hbm, values), (cot_hbm, cot),
                (embed_hbm, embed), (density_hbm, density), (weight_hbm, weight),
            )
        )
    ]
    for load in loads:
        load.start()
    barrier_signal()
    for load in loads[:3]:
        load.wait()
    make_payload(payload, values, cells, counts, table)
    halo_zero(fbufs)
    halo_zero(cbufs)
    loads[3].wait()
    barrier_wait()
    exchange_start(payload, recv, a2a_send, a2a_recv)
    halo_start(halo_copies(cot, cbufs, HC, cot_send, cot_recv))
    for load in loads[4:]:
        load.wait()

    def build(i, carry):
        lat = lax.rem(a - i + NA, NA)
        exchange_wait_recv(recv, a2a_recv, lat)
        rows = pl.ds(lat * NB * CAP, NB * CAP)
        codes = recv[pl.ds(lat * NB, NB), CAP : 2 * CAP, :].astype(F32).reshape(NB * CAP, F)
        cell = (codes[:, 0:1] * TC + codes[:, 64:65]).astype(jnp.int32)
        lane = lax.broadcasted_iota(jnp.int32, (NB * CAP, CELLS), 1)
        onehot[rows, :] = jnp.where(cell == lane, 1.0, 0.0).astype(BF16)
        return carry

    lax.fori_loop(0, NA, build, 0)
    both = jnp.concatenate([recv[:, 0:CAP, :].reshape(SLOTS, F), jnp.ones((SLOTS, F), BF16)], axis=1)
    sums = lax.dot_general(
        onehot[...], both, (((0,), (0,)), ((), ())), preferred_element_type=F32
    )
    numbers = sums[:, F:]
    divisor = jnp.maximum(numbers, 1.0)
    inv[...] = divisor
    cell_means = (sums[:, :F] / divisor).astype(BF16)
    means[...] = cell_means
    logs = jnp.log(1.0 + numbers)
    embedded = jnp.dot(cell_means, embed[...], preferred_element_type=F32) + jnp.concatenate(
        [logs, logs], axis=1
    ) * density[...]
    field[...] = embedded.astype(BF16).reshape(TR, TC, CH)
    halo_start(halo_copies(field, fbufs, HR, halo_send, halo_recv))
    halo_wait(cot, cbufs, HC, cot_send, cot_recv)
    for r in range(TR + 2 * HC):
        cot_ext[r] = ext_row(cot, cbufs, HC, r)
    halo_wait(field, fbufs, HR, halo_send, halo_recv)
    for r in range(TR + 2 * HR):
        put3(x0, slice(r, r + 1), ext_row(field, fbufs, HR, r))

    n = 11

    def fwd0(c, carry):
        pre = conv_fwd(x0, weight, 0, c * n, n)
        value, slope = gelu_parts(pre)
        old = x0[pl.ds(c * n + 1, n), :, CH : 2 * CH].reshape(n * W, CH).astype(F32)
        new = jnp.where(row_mask(a * TR - 3 + c * n, n), old + value, 0.0)
        new = new.astype(BF16).astype(F32)
        put3(x1, pl.ds(c * n, n), new)
        slope0[pl.ds(c * n, n)] = slope.reshape(n, W, CH)
        return carry

    lax.fori_loop(0, 2, fwd0, 0)
    m = 10

    def fwd1(c, carry):
        pre = conv_fwd(x1, weight, 1, c * m, m)
        value, slope = gelu_parts(pre)
        old = x1[pl.ds(c * m + 1, m), :, CH : 2 * CH].reshape(m * W, CH).astype(F32)
        grid2[pl.ds(c * m, m)] = (old + value).astype(BF16).reshape(m, W, CH)
        grad = cot_ext[pl.ds(c * m, m)].reshape(m * W, CH) * slope
        put3(g1, pl.ds(c * m, m), grad.astype(BF16).astype(F32))
        return carry

    lax.fori_loop(0, 2, fwd1, 0)

    grad1 = g1[2 : 2 + TR, :, CH : 2 * CH].reshape(TR * W, CH)
    kernel_grad(x1, 2, grad1, grads, 288, (1, 2))
    w1.pair_start()
    k = 9

    def bwd1(c, carry):
        up = conv_bwd(g1, weight, 1, c * k, k) + cot_ext[pl.ds(c * k + 1, k)].reshape(k * W, CH)
        up1[pl.ds(c * k, k)] = up.reshape(k, W, CH)
        grad = up * slope0[pl.ds(c * k + 2, k)].reshape(k * W, CH)
        grad = jnp.where(row_mask(a * TR - 1 + c * k, k), grad, 0.0)
        put3(g0, pl.ds(c * k, k), grad.astype(BF16).astype(F32))
        return carry

    lax.fori_loop(0, 2, bwd1, 0)
    w1.rs1_start()
    kernel_grad(x1, 2, grad1, grads, 288, (0,))
    kernel_grad(x0, 3, g0[1 : 1 + TR, :, CH : 2 * CH].reshape(TR * W, CH), grads, 0, (0, 1, 2))
    w2.pair_start()
    j = 8

    def bwd0(c, carry):
        up = conv_bwd(g0, weight, 0, c * j, j) + up1[pl.ds(c * j + 1, j)].reshape(j * W, CH)
        top[pl.ds(c * j, j)] = up.reshape(j, W, CH)[:, SIDE : SIDE + TC].astype(BF16)
        return carry

    lax.fori_loop(0, 2, bwd0, 0)
    w2.rs1_start()
    w1.rs2_start()
    top_grad = top[...].reshape(CELLS, CH)
    store_units(
        grads,
        EMBED0,
        lax.dot_general(
            means[...], top_grad, (((0,), (0,)), ((), ())), preferred_element_type=F32
        ),
    )
    es.pair_start()
    mean_grad = lax.dot_general(
        top_grad, embed[...], (((1,), (1,)), ((), ())), preferred_element_type=F32
    )
    scaled = (mean_grad / inv[...]).astype(BF16)
    picked[...] = jnp.dot(onehot[...], scaled, preferred_element_type=F32).astype(BF16).reshape(NT, CAP, F)
    out_ref[...] = grid2[2 : 2 + TR, SIDE : SIDE + TC, :]
    exchange_wait_send(payload, a2a_send)
    es.rs_start()
    w1.ag2_start()
    w2.rs2_start()
    exchange_start(picked, back, a2a_send, a2a_recv)
    es.sum_start()
    w1.ag1_start()
    w2.ag2_start()
    es.ag_start()
    w1.pair2_start()
    w2.ag1_start()
    es.pair2_start()
    w2.pair2_start()
    for lat in range(NA):
        exchange_wait_recv(back, a2a_recv, lat)
    exchange_wait_send(picked, a2a_send)
    w1.finish()
    w2.finish()
    es.finish()


VM = pl.BlockSpec(memory_space=pltpu.VMEM)
ANY = pl.BlockSpec(memory_space=pl.ANY)
DMA = pltpu.SemaphoreType.DMA


def vmem(shape, dtype=BF16):
    return pltpu.VMEM(shape, dtype)


def halo_shapes(rows):
    wide, side, corner = (rows, TC, CH), (TR, STRIP, CH), (rows, STRIP, CH)
    return [vmem(s) for s in (wide, wide, side, side, corner, corner, corner, corner)]


def wave_shapes(w):
    per = WAVES[w][1]
    units = 192 * per
    return [
        vmem((units, 8, 128)), vmem((units, 8, 128)), vmem((3, 3, 16 * per, 8, 128)),
        vmem((3, 16 * per, 8, 128)), vmem((3, 15, per, 8, 128)),
    ]


def body(obs_values, obs_cells, obs_counts, embed_weight, density_row, conv_weight, grid_cotangent):
    weight = conv_weight.reshape(2, 3, 3 * CH, CH)
    field, total, back = pl.pallas_call(
        kernel,
        out_shape=[
            jax.ShapeDtypeStruct((TR, TC, CH), BF16),
            jax.ShapeDtypeStruct((UNITS, 2, 8, 128), BF16),
            jax.ShapeDtypeStruct((NT, CAP, F), BF16),
        ],
        in_specs=[ANY] * 7,
        out_specs=[VM] * 3,
        scratch_shapes=[
            vmem((NT, CAP, F)), vmem((NT, CAP), jnp.int32), vmem((1, NT), jnp.int32), vmem((F, CH)),
            vmem((1, CH), F32), vmem((2, 3, 3 * CH, CH)), vmem((TR, TC, CH)), vmem((NT, F), F32),
            vmem((NT, 16, F)), vmem((NT, 16, F)), vmem((SLOTS, CELLS)), vmem((CELLS, F)), vmem((CELLS, F), F32),
            vmem((TR, TC, CH)), *halo_shapes(HR), *halo_shapes(HC),
            vmem((24, W, 3 * CH)), vmem((22, W, 3 * CH)), vmem((20, W, 3 * CH)), vmem((18, W, 3 * CH)),
            vmem((22, W, CH), F32), vmem((20, W, CH), F32), vmem((18, W, CH), F32),
            vmem((20, W, CH)), vmem((TR, TC, CH)), vmem((UNITS, 2, 8, 128)), vmem((NT, CAP, F)),
            *wave_shapes(0), *wave_shapes(1),
            vmem((16, 8, 128)), vmem((16, 8, 128)), vmem((15, 1, 8, 128)), vmem((1, 8, 128)), vmem((3, 1, 8, 128)),
            DMA((7,)), DMA, DMA((NA,)), DMA((8,)), DMA((8,)), DMA((8,)), DMA((8,)),
            DMA((2,)), DMA((3, 5, 2)), DMA((2,)), DMA((3, 5, 2)), DMA((5, 2)),
        ],
        compiler_params=pltpu.CompilerParams(
            collective_id=0, has_side_effects=True, vmem_limit_bytes=56 * 2**20
        ),
    )(
        obs_values[0], obs_cells[0], obs_counts, embed_weight, density_row.reshape(1, CH), weight, grid_cotangent
    )
    whole = total.transpose(0, 2, 1, 3).reshape(UNITS * 8, CH).astype(F32)
    grad_conv = whole[:4608].reshape(2, 3, 3, CH, CH)
    return field, grad_conv, whole[4608:], back[None]


def solution(mesh):
    return jax.shard_map(
        body,
        mesh=mesh,
        in_specs=(
            P(("lat", "lon"), None, None, None),
            P(("lat", "lon"), None, None),
            P(("lat", "lon"), None),
            P(),
            P(),
            P(),
            P("lat", "lon", None),
        ),
        out_specs=(P("lat", "lon", None), P(), P(), P(("lat", "lon"), None, None, None)),
        check_vma=False,
    )
```

time: 108 us -> 87.3 us (0.81)
  Pallas kernels: 96.5 us -> 78.4 us
  local copies, waits for them, and re-layouts: 7.44 us -> 6.03 us
  other arithmetic: 3.26 us -> 2.06 us
    pallas_call x2 -> x1, Pallas kernels: 96.5 us -> 78.4 us  [body(): pl.pallas_call(kernel, out_shape=[jax.ShapeDtypeStruct((TR, TC, CH), BF16...]
    concatenate x1 -> x0, other arithmetic: 1.84 us -> none  [body(): payload = jnp.concatenate([obs_values[0], codes], axis=1)]
    convert_element_type x1, other arithmetic: 0.38 us -> 2.06 us  [body(): whole = total.transpose(0, 2, 1, 3).reshape(UNITS * 8, CH).astype(F32)]
    unnamed x8 -> x7, local copies, waits for them, and re-layouts: 4.08 us -> 2.87 us
where the time goes in v2:
time: 87.3 us; the launch traced here: 87.1 us
  Pallas kernels  78.4 us (90%)
  local copies, waits for them, and re-layouts  6.03 us (7%)
  other arithmetic  2.06 us (2%)
    pallas_call x1, Pallas kernels, body(): pl.pallas_call(kernel, out_shape=[jax.ShapeDtypeStruct((TR, TC, CH), BF16...  78.4 us
    unnamed x7, local copies, waits for them, and re-layouts  2.87 us
    slice x1, local copies, waits for them, and re-layouts, body(): grad_conv = whole[:4608].reshape(2, 3, 3, CH, CH)  2.49 us
    convert_element_type x1, other arithmetic, body(): whole = total.transpose(0, 2, 1, 3).reshape(UNITS * 8, CH).astype(F32)  2.06 us

profile of v2, /device:TPU:1, one launch (start us, length us, event | category | flops | bytes accessed | tf_op | source)
XLA Modules:
  0.0 87.1 jit_solution(6140302315849112167)
XLA Ops:
  0.6 1.4 %copy.11 = s32[1,128,8]{2,1,0:T(8,128)} copy(s32[1,128,8]{1,2,0:T(8,128)} %param.8) | data formatting | bytes 8192 | tf_op args[1]
  2.0 78.4 %shard_map.102 = (bf16[16,48,256]{2,1,0:T(8,128)(2,1)}, bf16[592,2,8,128]{3,2,1,0:T(8,128)(2,1)}, bf16[128,8,128]{2,1,0:T(8,128)(2,1)}) custom-call(bf16[128,8,128]{2,1,0:T(8,128)(2,1)} %bitcast.12, s32[128,8]{1,0:T(8,128)} %bitcast.13, s32[1,128]{1,0:T(1,128)} %counts_hbm.1, bf16[128,256]{1,0:T(8,128)(2,1)} %embed_hbm.1, f32[1,256]{1,0:T(1,128)} %bitcast.15, ...), custom_call_target="tpu_custom_call" | custom-call | tf_op jit(solution)/shard_map/pallas_call | solution.py:637
  80.4 2.1 %convert_bitcast_fusion = f32[592,8,2,128]{3,1,2,0:T(8,128)S(1)} fusion(bf16[592,2,8,128]{3,2,1,0:T(8,128)(2,1)} %get-tuple-element.8), kind=kLoop, calls=%fused_computation | loop fusion | flops 1212416 | bytes 7274496 | tf_op jit(solution)/shard_map/convert_element_type | solution.py:665
  82.5 0.7 slice_bitcast_fusion
  83.2 0.0 copy-start
  83.2 0.0 copy-start.1
  83.2 2.5 %slice.13 = f32[576,8,2,128]{3,1,2,0:T(8,128)} slice(f32[592,8,2,128]{3,1,2,0:T(8,128)S(1)} %convert_bitcast_fusion), slice={[0:576], [0:8], [0:2], [0:128]} | slice | bytes 9437184 | tf_op jit(solution)/shard_map/slice | solution.py:666
  85.7 0.0 copy-done
  85.7 0.7 copy.14
  86.4 0.0 copy-done.1
  86.4 0.7 copy.15
Async XLA Ops:
  83.2 2.5 %copy-start = (bf16[16,48,256]{2,1,0:T(8,128)(2,1)S(1)}, bf16[16,48,256]{2,1,0:T(8,128)(2,1)}, u32[]{:S(2)}) copy-start(bf16[16,48,256]{2,1,0:T(8,128)(2,1)} %get-tuple-element.14) | copy-start | bytes 1179652
  83.2 3.2 %copy-start.1 = (bf16[128,8,128]{2,1,0:T(8,128)(2,1)S(1)}, bf16[128,8,128]{2,1,0:T(8,128)(2,1)}, u32[]{:S(2)}) copy-start(bf16[128,8,128]{2,1,0:T(8,128)(2,1)} %get-tuple-element.9) | copy-start | bytes 786436

commit v3 on v2

--- a/solution.py
+++ b/solution.py
@@ -210,12 +210,10 @@
 
 
 def kernel_grad(src, first, grad, dst, unit, taps_of):
-    col = lax.broadcasted_iota(jnp.int32, (TR * W, CH), 0) & (W - 1)
-    masked = jnp.where((col >= SIDE) & (col < SIDE + TC), grad.astype(F32), 0.0).astype(BF16)
     for p in taps_of:
-        window = src[first + p : first + p + TR].reshape(TR * W, 3 * CH)
+        window = src[first + p : first + p + TR, SIDE : SIDE + TC, :].reshape(CELLS, 3 * CH)
         taps = lax.dot_general(
-            window, masked, (((0,), (0,)), ((), ())), preferred_element_type=F32
+            window, grad, (((0,), (0,)), ((), ())), preferred_element_type=F32
         )
         store_units(dst, unit + p * 96, taps)
 
@@ -421,47 +419,149 @@
         wait_bytes(self.total.at[pl.ds(0, 16), c], self.sem.at[4, 1])
 
 
-def make_payload(payload, values, cells, counts, table):
-    eye = lax.broadcasted_iota(jnp.int32, (NT, NT), 0) == lax.broadcasted_iota(jnp.int32, (NT, NT), 1)
-    used = jnp.where(eye, counts[...].astype(F32), 0.0).sum(axis=1, keepdims=True)
-    slot = lax.broadcasted_iota(jnp.int32, (NT, CAP), 1).astype(F32)
+def make_table(table, cells, counts):
+    slot = lax.broadcasted_iota(jnp.int32, (CAP, NT), 0)
     cell = cells[...]
     row = (cell * 1366) >> 16
-    table[...] = jnp.zeros_like(table)
-    table[:, 0:CAP] = jnp.where(slot < used, row.astype(F32), -100.0)
-    table[:, CAP : 2 * CAP] = (cell - row * TC).astype(F32)
-    spread = jnp.broadcast_to(table[...][:, None, :], (NT, CAP, F)).reshape(SLOTS, F)
-    sub = lax.broadcasted_iota(jnp.int32, (SLOTS, F), 0) & (CAP - 1)
-    lane = lax.broadcasted_iota(jnp.int32, (SLOTS, F), 1)
-    spread = jnp.where((lane & (CAP - 1)) == sub, spread, 0.0).astype(BF16)
-    l0 = lax.broadcasted_iota(jnp.int32, (F, F), 0)
-    l1 = lax.broadcasted_iota(jnp.int32, (F, F), 1)
-    pick = ((l0 < CAP) & (l1 < 64)) | ((l0 >= CAP) & (l0 < 2 * CAP) & (l1 >= 64))
-    codes = jnp.dot(spread, jnp.where(pick, 1.0, 0.0).astype(BF16), preferred_element_type=F32)
-    payload[:, 0:CAP, :] = values[...]
-    payload[:, CAP : 2 * CAP, :] = codes.astype(BF16).reshape(NT, CAP, F)
+    table[0] = jnp.where(slot < counts[...], row, -100).astype(F32).astype(BF16)
+    table[1] = (cell - row * TC).astype(F32).astype(BF16)
+
+
+def to_group(fn, count):
+    def step(k, carry):
+        fn(k)
+        return carry
+
+    lax.fori_loop(1, count, step, 0)
+
+
+def codes_start(table, tables, sem):
+    a, b = coords()
+    pltpu.make_async_copy(table, tables.at[b], sem.at[1]).start()
+
+    def go(k):
+        pltpu.make_async_remote_copy(
+            src_ref=table, dst_ref=tables.at[b], send_sem=sem.at[0], recv_sem=sem.at[1],
+            device_id=(a, lax.rem(b + k, NB)), device_id_type=MESH,
+        ).start()
+
+    to_group(go, NB)
+
+
+def codes_forward(tables, mine, got, sem):
+    a, b = coords()
+    wait_bytes(tables, sem.at[1])
+    lat = lax.broadcasted_iota(jnp.int32, (NA, NT), 0)
+    tile = lax.broadcasted_iota(jnp.int32, (NA, NT), 1)
+    pick = jnp.where(tile == lat * NB + b, 1.0, 0.0).astype(BF16)
+    nt = (((1,), (1,)), ((), ()))
+    rows = lax.dot_general(pick, tables[:, 0].reshape(NB * CAP, NT), nt, preferred_element_type=F32)
+    cols = lax.dot_general(pick, tables[:, 1].reshape(NB * CAP, NT), nt, preferred_element_type=F32)
+    codes = rows * TC + cols
+    for i in range(NA):
+        mine[i] = codes[i : i + 1]
+    pltpu.make_async_copy(mine.at[a], got.at[a], sem.at[3]).start()
+
+    def go(k):
+        to = lax.rem(a + k, NA)
+        pltpu.make_async_remote_copy(
+            src_ref=mine.at[to], dst_ref=got.at[a], send_sem=sem.at[2], recv_sem=sem.at[3],
+            device_id=(to, b), device_id_type=MESH,
+        ).start()
+
+    to_group(go, NA)
+
+
+def place_codes(got, onehot, sem):
+    wait_bytes(got, sem.at[3])
+    rows = [got[i] for i in range(NA)] + [jnp.zeros((NT - NA, NT), F32)]
+    codes = jnp.concatenate(rows, axis=0).T
+    lane = lax.broadcasted_iota(jnp.int32, (NB * CAP, CELLS), 1).astype(F32)
+    for i in range(NA):
+        hit = codes[:, i : i + 1] == lane
+        onehot[i * NB * CAP : (i + 1) * NB * CAP, :] = jnp.where(hit, 1.0, 0.0).astype(BF16)
+
+
+def eye(dtype=None):
+    return lax.broadcasted_iota(jnp.int32, (128, 128), 0) == lax.broadcasted_iota(jnp.int32, (128, 128), 1)
+
+
+def pack_numbers(numbers, packed):
+    mask = eye()
+    for i in range(CELLS // 128):
+        packed[i : i + 1] = jnp.where(mask, numbers[i * 128 : (i + 1) * 128], 0.0).sum(axis=0, keepdims=True)
+
+
+def unpack_numbers(packed, first, count, out):
+    mask = eye()
+    ones = jnp.ones((256, 128), BF16)
+    for i in range(count):
+        row = packed[first + i : first + i + 1]
+        high = jnp.floor(row * 0.125) * 8.0
+        parts = [jnp.where(mask, jnp.broadcast_to(v, (128, 128)), 0.0).astype(BF16) for v in (high, row - high)]
+        out[i * 128 : (i + 1) * 128] = jnp.dot(
+            jnp.concatenate(parts, axis=1), ones, preferred_element_type=F32
+        )
+
+
+PACKED = {-1: (4, 2), 0: (0, 6), 1: (0, 2)}
+
+
+def numbers_row(own, bufs, r):
+    if r < HR:
+        left, mid, right, at = bufs[4], bufs[0], bufs[5], (TR - HR + r) * TC - 512
+    elif r < HR + TR:
+        left, mid, right, at = bufs[2], own, bufs[3], (r - HR) * TC
+    else:
+        left, mid, right, at = bufs[6], bufs[1], bufs[7], (r - HR - TR) * TC
+    return jnp.concatenate(
+        [left[at + TC - SIDE : at + TC], mid[at : at + TC], right[at : at + SIDE]], axis=0
+    )
+
+
+def packed_copies(packed, bufs, send, recv):
+    a, b = coords()
+    copies = []
+    for i, (da, db) in enumerate(DIRS):
+        back = DIRS.index((-da, -db))
+        copies.append(
+            pltpu.make_async_remote_copy(
+                src_ref=packed, dst_ref=bufs.at[back], send_sem=send.at[i], recv_sem=recv.at[back],
+                device_id=(jnp.clip(a + da, 0, NA - 1), lax.rem(b + db + NB, NB)), device_id_type=MESH,
+            )
+        )
+    return copies
+
+
+def waits(copies):
+    for i, (da, db) in enumerate(DIRS):
+        when_exists(da, copies[i].wait_send)
+        when_exists(da, copies[DIRS.index((-da, -db))].wait_recv)
 
 
 def kernel(
     values_hbm, cells_hbm, counts_hbm, embed_hbm, density_hbm, weight_hbm, cot_hbm,
     out_ref, total, back,
-    values, cells, counts, embed, density, weight, cot, table,
-    payload, recv, onehot, means, inv, field,
+    values, cells, counts, embed, density, weight, cot,
+    table, tables, codes_mine, codes_got, recv, onehot, means, numbers, packed, packs,
+    nN, nS, nW, nE, nNW, nNE, nSW, nSE,
     fN, fS, fW, fE, fNW, fNE, fSW, fSE,
     cN, cS, cW, cE, cNW, cNE, cSW, cSE,
     x0, x1, g1, g0, slope0, cot_ext, up1, grid2, top, grads, picked,
     *rest,
 ):
     w1_bufs, w2_bufs, e_bufs = rest[0:5], rest[5:10], rest[10:15]
-    (load_sem, a2a_send, a2a_recv, halo_send, halo_recv, cot_send, cot_recv,
+    (load_sem, a2a_send, a2a_recv, back_send, back_recv, code_sem, halo_send, halo_recv, pack_send, pack_recv, cot_send, cot_recv,
      w1_pair, w1_sem, w2_pair, w2_sem, e_sem) = rest[15:]
     a, _ = coords()
     pos = place()
     fbufs = (fN, fS, fW, fE, fNW, fNE, fSW, fSE)
+    nbufs = (nN, nS, nW, nE, nNW, nNE, nSW, nSE)
     cbufs = (cN, cS, cW, cE, cNW, cNE, cSW, cSE)
     w1 = Wave(0, pos, grads, total, w1_bufs, (w1_pair, w1_sem))
     w2 = Wave(1, pos, grads, total, w2_bufs, (w2_pair, w2_sem))
     es = EmbedSum(pos, grads, total, e_bufs, e_sem)
+    barrier_signal()
     loads = [
         pltpu.make_async_copy(src, dst, load_sem.at[i])
         for i, (src, dst) in enumerate(
@@ -473,51 +573,47 @@
     ]
     for load in loads:
         load.start()
-    barrier_signal()
+    halo_zero(fbufs)
+    halo_zero(cbufs)
+    halo_zero([packs.at[i] for i in range(8)])
+    packed[...] = jnp.zeros_like(packed)
     for load in loads[:3]:
         load.wait()
-    make_payload(payload, values, cells, counts, table)
-    halo_zero(fbufs)
-    halo_zero(cbufs)
-    loads[3].wait()
+    make_table(table, cells, counts)
     barrier_wait()
-    exchange_start(payload, recv, a2a_send, a2a_recv)
-    halo_start(halo_copies(cot, cbufs, HC, cot_send, cot_recv))
-    for load in loads[4:]:
+    codes_start(table, tables, code_sem)
+    exchange_start(values, recv, a2a_send, a2a_recv)
+    codes_forward(tables, codes_mine, codes_got, code_sem)
+    for load in loads[3:]:
         load.wait()
-
-    def build(i, carry):
-        lat = lax.rem(a - i + NA, NA)
+    place_codes(codes_got, onehot, code_sem)
+    for lat in range(NA):
         exchange_wait_recv(recv, a2a_recv, lat)
-        rows = pl.ds(lat * NB * CAP, NB * CAP)
-        codes = recv[pl.ds(lat * NB, NB), CAP : 2 * CAP, :].astype(F32).reshape(NB * CAP, F)
-        cell = (codes[:, 0:1] * TC + codes[:, 64:65]).astype(jnp.int32)
-        lane = lax.broadcasted_iota(jnp.int32, (NB * CAP, CELLS), 1)
-        onehot[rows, :] = jnp.where(cell == lane, 1.0, 0.0).astype(BF16)
-        return carry
-
-    lax.fori_loop(0, NA, build, 0)
-    both = jnp.concatenate([recv[:, 0:CAP, :].reshape(SLOTS, F), jnp.ones((SLOTS, F), BF16)], axis=1)
+    both = jnp.concatenate([recv[...].reshape(SLOTS, F), jnp.ones((SLOTS, F), BF16)], axis=1)
     sums = lax.dot_general(
         onehot[...], both, (((0,), (0,)), ((), ())), preferred_element_type=F32
     )
-    numbers = sums[:, F:]
-    divisor = jnp.maximum(numbers, 1.0)
-    inv[...] = divisor
-    cell_means = (sums[:, :F] / divisor).astype(BF16)
-    means[...] = cell_means
-    logs = jnp.log(1.0 + numbers)
-    embedded = jnp.dot(cell_means, embed[...], preferred_element_type=F32) + jnp.concatenate(
-        [logs, logs], axis=1
-    ) * density[...]
-    field[...] = embedded.astype(BF16).reshape(TR, TC, CH)
-    halo_start(halo_copies(field, fbufs, HR, halo_send, halo_recv))
-    halo_wait(cot, cbufs, HC, cot_send, cot_recv)
-    for r in range(TR + 2 * HC):
-        cot_ext[r] = ext_row(cot, cbufs, HC, r)
-    halo_wait(field, fbufs, HR, halo_send, halo_recv)
+    numbers[...] = sums[:, F:]
+    means[...] = (sums[:, :F] / jnp.maximum(sums[:, F:], 1.0)).astype(BF16).reshape(TR, TC, F)
+    pack_numbers(numbers, packed)
+    halo = halo_copies(means, fbufs, HR, halo_send, halo_recv)
+    packs_out = packed_copies(packed, packs, pack_send, pack_recv)
+    halo_start(packs_out)
+    halo_start(halo)
+    cot_halo = halo_copies(cot, cbufs, HC, cot_send, cot_recv)
+    halo_start(cot_halo)
+    waits(packs_out)
+    for i, (da, db) in enumerate(DIRS):
+        first, count = PACKED[da]
+        unpack_numbers(packs.at[i], first, count, nbufs[i])
+    waits(halo)
     for r in range(TR + 2 * HR):
-        put3(x0, slice(r, r + 1), ext_row(field, fbufs, HR, r))
+        mean_row = ext_row(means, fbufs, HR, r).astype(BF16)
+        logs = jnp.log(1.0 + numbers_row(numbers, nbufs, r))
+        embedded = jnp.dot(mean_row, embed[...], preferred_element_type=F32) + jnp.concatenate(
+            [logs, logs], axis=1
+        ) * density[...]
+        put3(x0, slice(r, r + 1), embedded.astype(BF16).astype(F32))
 
     n = 11
 
@@ -532,6 +628,9 @@
         return carry
 
     lax.fori_loop(0, 2, fwd0, 0)
+    waits(cot_halo)
+    for r in range(TR + 2 * HC):
+        cot_ext[r] = ext_row(cot, cbufs, HC, r)
     m = 10
 
     def fwd1(c, carry):
@@ -545,7 +644,7 @@
 
     lax.fori_loop(0, 2, fwd1, 0)
 
-    grad1 = g1[2 : 2 + TR, :, CH : 2 * CH].reshape(TR * W, CH)
+    grad1 = g1[2 : 2 + TR, SIDE : SIDE + TC, CH : 2 * CH].reshape(CELLS, CH)
     kernel_grad(x1, 2, grad1, grads, 288, (1, 2))
     w1.pair_start()
     k = 9
@@ -561,7 +660,7 @@
     lax.fori_loop(0, 2, bwd1, 0)
     w1.rs1_start()
     kernel_grad(x1, 2, grad1, grads, 288, (0,))
-    kernel_grad(x0, 3, g0[1 : 1 + TR, :, CH : 2 * CH].reshape(TR * W, CH), grads, 0, (0, 1, 2))
+    kernel_grad(x0, 3, g0[1 : 1 + TR, SIDE : SIDE + TC, CH : 2 * CH].reshape(CELLS, CH), grads, 0, (0, 1, 2))
     w2.pair_start()
     j = 8
 
@@ -572,43 +671,65 @@
 
     lax.fori_loop(0, 2, bwd0, 0)
     w2.rs1_start()
-    w1.rs2_start()
     top_grad = top[...].reshape(CELLS, CH)
+    mean_rows = means[...].reshape(CELLS, F)
     store_units(
         grads,
         EMBED0,
-        lax.dot_general(
-            means[...], top_grad, (((0,), (0,)), ((), ())), preferred_element_type=F32
-        ),
+        lax.dot_general(mean_rows, top_grad, (((0,), (0,)), ((), ())), preferred_element_type=F32),
     )
     es.pair_start()
     mean_grad = lax.dot_general(
         top_grad, embed[...], (((1,), (1,)), ((), ())), preferred_element_type=F32
     )
-    scaled = (mean_grad / inv[...]).astype(BF16)
+    scaled = (mean_grad / jnp.maximum(numbers[...], 1.0)).astype(BF16)
     picked[...] = jnp.dot(onehot[...], scaled, preferred_element_type=F32).astype(BF16).reshape(NT, CAP, F)
     out_ref[...] = grid2[2 : 2 + TR, SIDE : SIDE + TC, :]
-    exchange_wait_send(payload, a2a_send)
+    w1.rs2_start()
     es.rs_start()
+    w2.rs2_start()
+    exchange_start(picked, back, back_send, back_recv)
     w1.ag2_start()
-    w2.rs2_start()
-    exchange_start(picked, back, a2a_send, a2a_recv)
     es.sum_start()
+    w2.ag2_start()
     w1.ag1_start()
-    w2.ag2_start()
     es.ag_start()
+    w2.ag1_start()
     w1.pair2_start()
-    w2.ag1_start()
     es.pair2_start()
     w2.pair2_start()
     for lat in range(NA):
-        exchange_wait_recv(back, a2a_recv, lat)
-    exchange_wait_send(picked, a2a_send)
+        exchange_wait_recv(back, back_recv, lat)
+    exchange_wait_send(values, a2a_send)
+    exchange_wait_send(picked, back_send)
+    wait_bytes(tables.at[pl.ds(0, NB - 1)], code_sem.at[0])
+    wait_bytes(codes_got.at[pl.ds(0, NA - 1)], code_sem.at[2])
     w1.finish()
     w2.finish()
     es.finish()
 
 
+def write_kernel(total, field, back, conv_out, embed_out, field_out, back_out, wide, sem):
+    copies = [
+        pltpu.make_async_copy(field, field_out, sem.at[0]),
+        pltpu.make_async_copy(back, back_out, sem.at[1]),
+    ]
+    for copy in copies:
+        copy.start()
+    bounds = [64 * i for i in range(10)] + [UNITS]
+    for i, (u0, u1) in enumerate(zip(bounds, bounds[1:])):
+        rows = pl.ds(u0 * 8, (u1 - u0) * 8)
+        for h in range(2):
+            part = total[u0:u1, h].astype(F32).reshape((u1 - u0) * 8, 128)
+            wide[rows, h * 128 : (h + 1) * 128] = part
+        dst = embed_out if u0 == EMBED0 else conv_out.at[rows]
+        copy = pltpu.make_async_copy(wide.at[rows], dst, sem.at[2 + i])
+        copy.start()
+        copies.append(copy)
+    for copy in copies:
+        copy.wait()
+
+
 VM = pl.BlockSpec(memory_space=pltpu.VMEM)
 ANY = pl.BlockSpec(memory_space=pl.ANY)
 DMA = pltpu.SemaphoreType.DMA
@@ -618,8 +739,8 @@
     return pltpu.VMEM(shape, dtype)
 
 
-def halo_shapes(rows):
-    wide, side, corner = (rows, TC, CH), (TR, STRIP, CH), (rows, STRIP, CH)
+def halo_shapes(rows, width):
+    wide, side, corner = (rows, TC, width), (TR, STRIP, width), (rows, STRIP, width)
     return [vmem(s) for s in (wide, wide, side, side, corner, corner, corner, corner)]
 
 
@@ -634,6 +755,7 @@
 
 def body(obs_values, obs_cells, obs_counts, embed_weight, density_row, conv_weight, grid_cotangent):
     weight = conv_weight.reshape(2, 3, 3 * CH, CH)
+    args = (obs_values[0], obs_cells[0].T, obs_counts, embed_weight, density_row.reshape(1, CH), weight, grid_cotangent)
     field, total, back = pl.pallas_call(
         kernel,
         out_shape=[
@@ -644,27 +766,39 @@
         in_specs=[ANY] * 7,
         out_specs=[VM] * 3,
         scratch_shapes=[
-            vmem((NT, CAP, F)), vmem((NT, CAP), jnp.int32), vmem((1, NT), jnp.int32), vmem((F, CH)),
-            vmem((1, CH), F32), vmem((2, 3, 3 * CH, CH)), vmem((TR, TC, CH)), vmem((NT, F), F32),
-            vmem((NT, 16, F)), vmem((NT, 16, F)), vmem((SLOTS, CELLS)), vmem((CELLS, F)), vmem((CELLS, F), F32),
-            vmem((TR, TC, CH)), *halo_shapes(HR), *halo_shapes(HC),
+            vmem((NT, CAP, F)), vmem((CAP, NT), jnp.int32), vmem((1, NT), jnp.int32), vmem((F, CH)),
+            vmem((1, CH), F32), vmem((2, 3, 3 * CH, CH)), vmem((TR, TC, CH)),
+            vmem((2, CAP, NT)), vmem((NB, 2, CAP, NT)), vmem((NA, 1, NT), F32), vmem((NA, 1, NT), F32),
+            vmem((NT, CAP, F)), vmem((SLOTS, CELLS)), vmem((TR, TC, F)), vmem((CELLS, F), F32),
+            vmem((8, 128), F32), vmem((8, 8, 128), F32),
+            *[vmem((PACKED[da][1] * 128, 128), F32) for da, _ in DIRS],
+            *halo_shapes(HR, F), *halo_shapes(HC, CH),
             vmem((24, W, 3 * CH)), vmem((22, W, 3 * CH)), vmem((20, W, 3 * CH)), vmem((18, W, 3 * CH)),
             vmem((22, W, CH), F32), vmem((20, W, CH), F32), vmem((18, W, CH), F32),
             vmem((20, W, CH)), vmem((TR, TC, CH)), vmem((UNITS, 2, 8, 128)), vmem((NT, CAP, F)),
             *wave_shapes(0), *wave_shapes(1),
             vmem((16, 8, 128)), vmem((16, 8, 128)), vmem((15, 1, 8, 128)), vmem((1, 8, 128)), vmem((3, 1, 8, 128)),
-            DMA((7,)), DMA, DMA((NA,)), DMA((8,)), DMA((8,)), DMA((8,)), DMA((8,)),
+            DMA((7,)), DMA, DMA((NA,)), DMA, DMA((NA,)), DMA((4,)), DMA((8,)), DMA((8,)), DMA((8,)), DMA((8,)), DMA((8,)), DMA((8,)),
             DMA((2,)), DMA((3, 5, 2)), DMA((2,)), DMA((3, 5, 2)), DMA((5, 2)),
         ],
         compiler_params=pltpu.CompilerParams(
-            collective_id=0, has_side_effects=True, vmem_limit_bytes=56 * 2**20
+            collective_id=0, has_side_effects=True, vmem_limit_bytes=40 * 2**20
         ),
-    )(
-        obs_values[0], obs_cells[0], obs_counts, embed_weight, density_row.reshape(1, CH), weight, grid_cotangent
-    )
-    whole = total.transpose(0, 2, 1, 3).reshape(UNITS * 8, CH).astype(F32)
-    grad_conv = whole[:4608].reshape(2, 3, 3, CH, CH)
-    return field, grad_conv, whole[4608:], back[None]
+    )(*[pltpu.with_memory_space_constraint(arg, pltpu.HBM) for arg in args])
+    grad_conv, grad_embed, field, back = pl.pallas_call(
+        write_kernel,
+        out_shape=[
+            jax.ShapeDtypeStruct((EMBED0 * 8, CH), F32),
+            jax.ShapeDtypeStruct((F, CH), F32),
+            jax.ShapeDtypeStruct(field.shape, BF16),
+            jax.ShapeDtypeStruct(back.shape, BF16),
+        ],
+        in_specs=[VM] * 3,
+        out_specs=[ANY] * 4,
+        scratch_shapes=[vmem((UNITS * 8, CH), F32), DMA((12,))],
+        compiler_params=pltpu.CompilerParams(vmem_limit_bytes=20 * 2**20),
+    )(total, field, back)
+    return field, grad_conv.reshape(2, 3, 3, CH, CH), grad_embed, back[None]
 
 
 def solution(mesh):

time: 87.3 us -> 71.2 us (0.82)
  Pallas kernels: 78.4 us -> 70.4 us
  local copies, waits for them, and re-layouts: 6.03 us -> 0 us
  other arithmetic: 2.06 us -> 0 us
    pallas_call x1, Pallas kernels: 78.4 us -> 67.9 us  [body(): pl.pallas_call(kernel, out_shape=[jax.ShapeDtypeStruct((TR, TC, CH), BF16...]
    slice x2 -> x0, local copies, waits for them, and re-layouts: 3.15 us -> none  [the longest x1 2.49 us: body(): grad_conv = whole[:4608].reshape(2, 3, 3, CH, CH)]
    unnamed x7 -> x0, local copies, waits for them, and re-layouts: 2.87 us -> none
    pallas_call x0 -> x1, Pallas kernels: none -> 2.5 us  [body(): pl.pallas_call(write_kernel, out_shape=[jax.ShapeDtypeStruct((EMBED0 * 8,...]
    convert_element_type x1 -> x0, other arithmetic: 2.06 us -> none  [body(): whole = total.transpose(0, 2, 1, 3).reshape(UNITS * 8, CH).astype(F32)]
where the time goes in v3:
time: 71.2 us; the launch traced here: 71.1 us
  Pallas kernels  70.4 us (99%)
    pallas_call x1, Pallas kernels, body(): pl.pallas_call(kernel, out_shape=[jax.ShapeDtypeStruct((TR, TC, CH), BF16...  67.9 us
    pallas_call x1, Pallas kernels, body(): pl.pallas_call(write_kernel, out_shape=[jax.ShapeDtypeStruct((EMBED0 * 8,...  2.5 us

profile of v3, /device:TPU:1, one launch (start us, length us, event | category | flops | bytes accessed | tf_op | source)
XLA Modules:
  0.0 71.1 jit_solution(15678060716385931375)
XLA Ops:
  0.6 67.9 %shard_map.102 = (bf16[16,48,256]{2,1,0:T(8,128)(2,1)S(1)}, bf16[592,2,8,128]{3,2,1,0:T(8,128)(2,1)S(1)}, bf16[128,8,128]{2,1,0:T(8,128)(2,1)S(1)}) custom-call(bf16[128,8,128]{2,1,0:T(8,128)(2,1)} %bitcast.9, s32[8,128]{1,0:T(8,128)} %bitcast.10, s32[1,128]{1,0:T(1,128)} %counts_hbm.1, bf16[128,256]{1,0:T(8,128)(2,1)} %embed_hbm.1, f32[1,256]{1,0:T(1,128)} %bitcast.11, ...), custom_call_target="tpu_custom_call" | custom-call | tf_op jit(solution)/shard_map/pallas_call | solution.py:759
  68.6 2.5 %shard_map.103 = (f32[4608,256]{1,0:T(8,128)}, f32[128,256]{1,0:T(8,128)}, bf16[16,48,256]{2,1,0:T(8,128)(2,1)}, bf16[128,8,128]{2,1,0:T(8,128)(2,1)}) custom-call(bf16[592,2,8,128]{3,2,1,0:T(8,128)(2,1)S(1)} %get-tuple-element.11.total, bf16[16,48,256]{2,1,0:T(8,128)(2,1)S(1)} %get-tuple-element.12.field, bf16[128,8,128]{2,1,0:T(8,128)(2,1)S(1)} %get-tuple-element.13.back), custom_call_target="tpu_custom_call" | custom-call | tf_op jit(solution)/shard_map/pallas_call | solution.py:788

commit v4 on v3

--- a/solution.py
+++ b/solution.py
@@ -18,7 +18,7 @@
 HC = 2
 SIDE = 8
 W = TC + 2 * SIDE
-STRIP = 16
+POOL = 1536
 UNITS = 592
 F32, BF16 = jnp.float32, jnp.bfloat16
 GC, GA = 0.7978845608028654, 0.044715
@@ -32,47 +32,53 @@
     return (t // NB, lax.rem(t, NB))
 
 
+FAR_Z = (2, 1, 3, 0)
+
+
+def all_others(fn, planes=FAR_Z):
+    a, b = coords()
+    z, hi = a // 2, lax.rem(a, 2)
+    for dz in planes:
+        for dh in (1, 0):
+            lat = lax.rem(z + dz, 4) * 2 + lax.rem(hi + dh, 2)
+
+            def step(k, carry, lat=lat):
+                fn(lat, lax.rem(b + k, NB))
+                return carry
+
+            lax.fori_loop(0 if dz or dh else 1, NB, step, 0)
+
+
 def barrier_signal():
+    sem = pltpu.get_barrier_semaphore()
+    all_others(lambda lat, lon: pl.semaphore_signal(sem, inc=1, device_id=(lat, lon), device_id_type=MESH))
+
+
+def barrier_wait():
+    pl.semaphore_wait(pltpu.get_barrier_semaphore(), NT - 1)
+
+
+def exchange_own(src, dst, recv):
     a, b = coords()
     me = a * NB + b
-    sem = pltpu.get_barrier_semaphore()
-
-    def signal(k, carry):
-        t = lax.rem(me + k, NT)
-        pl.semaphore_signal(sem, inc=1, device_id=tile_dev(t), device_id_type=MESH)
-        return carry
-
-    lax.fori_loop(1, NT, signal, 0)
-
-
-def barrier_wait():
-    pl.semaphore_wait(pltpu.get_barrier_semaphore(), NT - 1)
-
-
-def exchange_start(src, dst, send, recv):
+    pltpu.make_async_copy(src.at[me], dst.at[me], recv).start()
+
+
+def exchange_start(src, dst, send, recv, planes):
     a, b = coords()
     me = a * NB + b
 
-    def go(k, carry):
-        ta = lax.rem(a + k // NB, NA)
-        tb = lax.rem(b + lax.rem(k, NB), NB)
+    def go(lat, lon):
         pltpu.make_async_remote_copy(
-            src_ref=src.at[ta * NB + tb],
+            src_ref=src.at[lat * NB + lon],
             dst_ref=dst.at[me],
             send_sem=send,
-            recv_sem=recv.at[a],
-            device_id=(ta, tb),
+            recv_sem=recv,
+            device_id=(lat, lon),
             device_id_type=MESH,
         ).start()
-        return carry
-
-    pltpu.make_async_copy(src.at[me], dst.at[me], recv.at[a]).start()
-    lax.fori_loop(1, NT, go, 0)
-
-
-def exchange_wait_recv(dst, recv, lat):
-    part = dst.at[pl.ds(lat * NB, NB)]
-    pltpu.make_async_copy(part, part, recv.at[lat]).wait()
+
+    all_others(go, planes)
 
 
 def exchange_wait_send(src, send):
@@ -83,61 +89,84 @@
 DIRS = [(-1, 0), (1, 0), (0, -1), (0, 1), (-1, -1), (-1, 1), (1, -1), (1, 1)]
 
 
-def halo_copies(src, bufs, rows, send, recv):
+def make_strips(src, strips):
+    strips[0] = src[:, 0:SIDE, :]
+    strips[1] = src[:, TC - SIDE : TC, :]
+
+
+def make_pairs(src, pairs):
+    for side, at in ((0, 0), (1, TC - 8)):
+        cut = slice(0, HC) if side == 0 else slice(8 - HC, 8)
+        for i in range(TR // 4):
+            parts = [src[4 * i + j, at : at + 8].astype(F32)[cut] for j in range(4)]
+            pairs[side, i] = jnp.concatenate(parts, axis=0).astype(BF16)
+
+
+def pairs_start(src, pairs, bufs, send, recv):
+    for da, db in DIRS:
+        back = DIRS.index((-da, -db))
+        if db == 0:
+            part = src.at[pl.ds(0, HC) if da < 0 else pl.ds(TR - HC, HC)]
+        else:
+            blocks = {-1: pl.ds(0, 1), 0: pl.ds(0, TR // 4), 1: pl.ds(TR // 4 - 1, 1)}[da]
+            part = pairs.at[(db + 1) // 2, blocks]
+        pltpu.make_async_remote_copy(
+            src_ref=part, dst_ref=bufs[back], send_sem=send, recv_sem=recv,
+            device_id=neighbour(da, db), device_id_type=MESH,
+        ).start()
+
+
+PAIR_UNITS = (2 * HC * TC + 2 * TR * 2 + 4 * 8) * CH // 1024
+
+
+def pairs_row(core, bufs, r):
+    if r < HC:
+        left, mid, right = bufs[4][0], bufs[0][r], bufs[5][0]
+        at = 8 - 2 * HC + HC * r
+    elif r < HC + TR:
+        k = r - HC
+        left, mid, right = bufs[2][k // 4], core[k], bufs[3][k // 4]
+        at = HC * (k % 4)
+    else:
+        k = r - HC - TR
+        left, mid, right = bufs[6][0], bufs[1][k], bufs[7][0]
+        at = HC * k
+    zero = jnp.zeros((SIDE - HC, CH), F32)
+    return jnp.concatenate(
+        [zero, left.astype(F32)[at : at + HC], mid.astype(F32), right.astype(F32)[at : at + HC], zero], axis=0
+    )
+
+
+def neighbour(da, db):
     a, b = coords()
-    copies = []
-    for i, (da, db) in enumerate(DIRS):
+    return (lax.rem(a + da + NA, NA), lax.rem(b + db + NB, NB))
+
+
+def halo_start(src, strips, bufs, rows, send, recv):
+    for da, db in DIRS:
         back = DIRS.index((-da, -db))
         row = {-1: pl.ds(0, rows), 0: pl.ds(0, TR), 1: pl.ds(TR - rows, rows)}[da]
-        col = {-1: pl.ds(0, STRIP), 0: pl.ds(0, TC), 1: pl.ds(TC - STRIP, STRIP)}[db]
-        copies.append(
-            pltpu.make_async_remote_copy(
-                src_ref=src.at[row, col],
-                dst_ref=bufs[back],
-                send_sem=send.at[i],
-                recv_sem=recv.at[back],
-                device_id=(
-                    jnp.clip(a + da, 0, NA - 1),
-                    lax.rem(b + db + NB, NB),
-                ),
-                device_id_type=MESH,
-            )
-        )
-    return copies
-
-
-def when_exists(da, fn):
+        whole = src if db == 0 else strips.at[(db + 1) // 2]
+        pltpu.make_async_remote_copy(
+            src_ref=whole.at[row], dst_ref=bufs[back], send_sem=send, recv_sem=recv,
+            device_id=neighbour(da, db), device_id_type=MESH,
+        ).start()
+
+
+def halo_units(rows, width):
+    return (2 * rows * TC + 2 * TR * SIDE + 4 * rows * SIDE) * width // 1024
+
+
+def halo_zero(bufs):
     a, _ = coords()
-    if da == 0:
-        fn()
-    elif da < 0:
-        pl.when(a > 0)(fn)
-    else:
-        pl.when(a < NA - 1)(fn)
-
-
-def halo_start(copies):
-    for (da, _), copy in zip(DIRS, copies):
-        when_exists(da, copy.start)
-
-
-def halo_wait(src, bufs, rows, send, recv):
-    copies = halo_copies(src, bufs, rows, send, recv)
-    for i, (da, db) in enumerate(DIRS):
-        when_exists(da, copies[i].wait_send)
-        back = DIRS.index((-da, -db))
-        when_exists(da, copies[back].wait_recv)
-
-
-def halo_zero(bufs):
-    for i, (da, _) in enumerate(DIRS):
-        if da:
-
-            def clear(buf=bufs[i]):
-                buf[...] = jnp.zeros(buf.shape, buf.dtype)
-
-            a, _ = coords()
-            pl.when(a == (0 if da < 0 else NA - 1))(clear)
+    for end, at in ((0, -1), (NA - 1, 1)):
+
+        def clear(at=at):
+            for i, (da, _) in enumerate(DIRS):
+                if da == at:
+                    bufs[i][...] = jnp.zeros(bufs[i].shape, bufs[i].dtype)
+
+        pl.when(a == end)(clear)
 
 
 def ext_row(core, bufs, rows, r):
@@ -149,9 +178,9 @@
         left, mid, right, k = bufs[6], bufs[1], bufs[7], r - rows - TR
     return jnp.concatenate(
         [
-            left[k].astype(F32)[STRIP - SIDE :],
+            left[k].astype(F32),
             mid[k].astype(F32),
-            right[k].astype(F32)[:SIDE],
+            right[k].astype(F32),
         ],
         axis=0,
     )
@@ -273,46 +302,45 @@
 
 
 class Wave:
-    def __init__(self, w, pos, grads, total, bufs, sems):
+    def __init__(self, w, pos, grads, total, bufs, sem, pool):
         self.first, self.per = WAVES[w]
-        self.pos, self.grads, self.total = pos, grads, total
-        self.pair, self.own, self.r1, self.t1, self.r2 = bufs
-        self.pair_sem, self.sem = sems
+        self.pos, self.grads, self.total, self.pool = pos, grads, total, pool
+        self.pair, self.own, self.r1, self.t1, self.r2, self.t2 = bufs
         self.stream = 64 * self.per
-
-    def send(self, s, phase):
-        return self.sem.at[s, phase, 0]
-
-    def recv(self, s, phase):
-        return self.sem.at[s, phase, 1]
-
-    def mine(self):
-        return self.grads.at[pl.ds(self.first, 3 * self.stream), 1 - self.pos["c"]]
+        self.send, self.pair_got, self.back_got = sem.at[0], sem.at[1], sem.at[2]
+        self.got1 = [sem.at[3 + s] for s in range(3)]
+        self.got2 = [sem.at[6 + s] for s in range(3)]
+        self.got3 = [sem.at[9 + s] for s in range(3)]
+        self.got4 = {step: sem.at[11 + step] for step in (1, 2, 3)}
+
+    def wait(self, units, sem):
+        wait_bytes(self.pool.at[pl.ds(0, units * self.per)], sem)
 
     def pair_start(self):
-        remote(self.mine(), self.pair, self.pair_sem.at[0], self.pair_sem.at[1], other_core(self.pos))
+        mine = self.grads.at[pl.ds(self.first, 3 * self.stream), 1 - self.pos["c"]]
+        remote(mine, self.pair, self.send, self.pair_got, other_core(self.pos))
 
     def rs1_start(self):
         pos, part = self.pos, 16 * self.per
-        wait_bytes(self.pair, self.pair_sem.at[1])
+        wait_bytes(self.pair, self.pair_got)
         kept = self.grads[pl.ds(self.first, 3 * self.stream), pos["c"]]
         self.own[...] = (kept.astype(F32) + self.pair[...].astype(F32)).astype(BF16)
         for step in (2, 1, 3):
             for s, order in enumerate(ORDERS):
                 peer = along(pos, order[0], step)
                 src = self.own.at[pl.ds(s * self.stream + peer[order[0]] * part, part)]
-                remote(src, self.r1.at[s, step - 1], self.send(s, 0), self.recv(s, 0), peer)
+                remote(src, self.r1.at[s, step - 1], self.send, self.got1[s], peer)
 
     def rs2_start(self):
         pos, part, per = self.pos, 16 * self.per, self.per
         for s, order in enumerate(ORDERS):
-            wait_bytes(self.r1.at[s], self.recv(s, 0))
+            wait_bytes(self.r1.at[s], self.got1[s])
             kept = self.own[pl.ds(s * self.stream + pos[order[0]] * part, part)]
             self.t1[s] = add_parts(kept, self.r1.at[s], 3)
 
             def go(peer, k, s=s, order=order):
                 src = self.t1.at[s, pl.ds((peer[order[1]] * 4 + peer[order[2]]) * per, per)]
-                remote(src, self.r2.at[s, k], self.send(s, 1), self.recv(s, 1), peer)
+                remote(src, self.r2.at[s, k], self.send, self.got2[s], peer)
 
             on_plane(pos, order[1:], go)
 
@@ -324,74 +352,73 @@
     def ag2_start(self):
         pos, per, c = self.pos, self.per, self.pos["c"]
         for s, order in enumerate(ORDERS):
-            wait_bytes(self.r2.at[s], self.recv(s, 1))
+            wait_bytes(self.r2.at[s], self.got2[s])
             start, inner = self.block(s, order)
-            self.total[pl.ds(start + inner, per), c] = add_parts(
-                self.t1[s, pl.ds(inner, per)], self.r2.at[s], 15
-            )
+            self.t2[s] = add_parts(self.t1[s, pl.ds(inner, per)], self.r2.at[s], 15)
             block = self.total.at[pl.ds(start + inner, per), c]
+            pltpu.make_async_copy(self.t2.at[s], block, self.got3[s]).start()
 
             def go(peer, k, s=s, block=block):
-                remote(block, block, self.send(s, 2), self.recv(s, 2), peer)
+                remote(self.t2.at[s], block, self.send, self.got3[s], peer)
 
             on_plane(pos, order[1:], go)
 
     def ag1_start(self):
         pos, per, c = self.pos, self.per, self.pos["c"]
         for s, order in enumerate(ORDERS):
-            wait_bytes(self.total.at[pl.ds(0, 15 * per), c], self.recv(s, 2))
+            self.wait(16, self.got3[s])
             start, _ = self.block(s, order)
             block = self.total.at[pl.ds(start, 16 * per), c]
             for step in (2, 1, 3):
-                remote(block, block, self.send(s, 3), self.recv(s, 3), along(pos, order[0], step))
+                remote(block, block, self.send, self.got4[step], along(pos, order[0], step))
+            remote(block, block, self.send, self.back_got, other_core(pos))
 
     def pair2_start(self):
-        c = self.pos["c"]
-        for s in range(3):
-            wait_bytes(self.total.at[pl.ds(0, 48 * self.per), c], self.recv(s, 3))
-            block = self.total.at[pl.ds(self.first + s * self.stream, self.stream), c]
-            remote(block, block, self.send(s, 4), self.recv(s, 4), other_core(self.pos))
+        pos, part, c = self.pos, 16 * self.per, self.pos["c"]
+        for step in (1, 3, 2):
+            self.wait(48, self.got4[step])
+            for s, order in enumerate(ORDERS):
+                came = lax.rem(pos[order[0]] + 4 - step, 4)
+                block = self.total.at[pl.ds(self.first + s * self.stream + came * part, part), c]
+                remote(block, block, self.send, self.back_got, other_core(pos))
 
     def finish(self):
-        c, per = self.pos["c"], self.per
-        wait_bytes(self.pair, self.pair_sem.at[0])
-        for s in range(3):
-            for phase, units in enumerate((48, 15, 15, 48, 64)):
-                wait_bytes(self.total.at[pl.ds(0, units * per), c], self.send(s, phase))
-            wait_bytes(self.total.at[pl.ds(0, self.stream), c], self.recv(s, 4))
+        self.wait(192 + 3 * (48 + 15 + 15 + 48 + 16 + 48), self.send)
+        self.wait(192, self.back_got)
 
 
 class EmbedSum:
-    def __init__(self, pos, grads, total, bufs, sem):
-        self.pos, self.grads, self.total, self.sem = pos, grads, total, sem
-        self.pair, self.own, self.r1, self.t1, self.r2 = bufs
+    def __init__(self, pos, grads, total, bufs, sem, pool):
+        self.pos, self.grads, self.total, self.pool = pos, grads, total, pool
+        self.pair, self.own, self.r1, self.t1, self.r2, self.t2 = bufs
+        self.send, self.got = sem.at[0], [sem.at[1 + i] for i in range(5)]
 
     def pair_start(self):
         src = self.grads.at[pl.ds(EMBED0, EMBED_UNITS), 1 - self.pos["c"]]
-        remote(src, self.pair, self.sem.at[0, 0], self.sem.at[0, 1], other_core(self.pos))
+        remote(src, self.pair, self.send, self.got[0], other_core(self.pos))
 
     def rs_start(self):
         pos = self.pos
-        wait_bytes(self.pair, self.sem.at[0, 1])
+        wait_bytes(self.pair, self.got[0])
         kept = self.grads[pl.ds(EMBED0, EMBED_UNITS), pos["c"]]
         self.own[...] = (kept.astype(F32) + self.pair[...].astype(F32)).astype(BF16)
 
         def go(peer, k):
             src = self.own.at[pl.ds(peer["y"] * 4 + peer["z"], 1)]
-            remote(src, self.r1.at[k], self.sem.at[1, 0], self.sem.at[1, 1], peer)
+            remote(src, self.r1.at[k], self.send, self.got[1], peer)
 
         on_plane(pos, ("y", "z"), go)
 
     def sum_start(self):
         pos = self.pos
-        wait_bytes(self.r1, self.sem.at[1, 1])
+        wait_bytes(self.r1, self.got[1])
         self.t1[...] = add_parts(self.own[pl.ds(pos["y"] * 4 + pos["z"], 1)], self.r1, 15)
         for step in range(1, 4):
-            remote(self.t1, self.r2.at[step - 1], self.sem.at[2, 0], self.sem.at[2, 1], along(pos, "x", step))
+            remote(self.t1, self.r2.at[step - 1], self.send, self.got[2], along(pos, "x", step))
 
     def ag_start(self):
         pos, c = self.pos, self.pos["c"]
-        wait_bytes(self.r2, self.sem.at[2, 1])
+        wait_bytes(self.r2, self.got[2])
         at = EMBED0 + pos["y"] * 4 + pos["z"]
         parts = []
         for i in range(4):
@@ -399,24 +426,20 @@
             for step in range(1, 4):
                 got = jnp.where(lax.rem(pos["x"] - step + 4, 4) == i, self.r2[step - 1].astype(F32), got)
             parts.append(got)
-        self.total[pl.ds(at, 1), c] = (((parts[0] + parts[1]) + parts[2]) + parts[3]).astype(BF16)
+        self.t2[...] = (((parts[0] + parts[1]) + parts[2]) + parts[3]).astype(BF16)
         block = self.total.at[pl.ds(at, 1), c]
-        on_plane(
-            pos, ("y", "z"),
-            lambda peer, k: remote(block, block, self.sem.at[3, 0], self.sem.at[3, 1], peer),
-        )
+        pltpu.make_async_copy(self.t2, block, self.got[3]).start()
+        on_plane(pos, ("y", "z"), lambda peer, k: remote(self.t2, block, self.send, self.got[3], peer))
 
     def pair2_start(self):
         c = self.pos["c"]
-        wait_bytes(self.total.at[pl.ds(0, 15), c], self.sem.at[3, 1])
+        wait_bytes(self.pool.at[pl.ds(0, 16)], self.got[3])
         block = self.total.at[pl.ds(EMBED0, EMBED_UNITS), c]
-        remote(block, block, self.sem.at[4, 0], self.sem.at[4, 1], other_core(self.pos))
+        remote(block, block, self.send, self.got[4], other_core(self.pos))
 
     def finish(self):
-        c = self.pos["c"]
-        for phase, units in enumerate((16, 15, 3, 15, 16)):
-            wait_bytes(self.total.at[pl.ds(0, units), c], self.sem.at[phase, 0])
-        wait_bytes(self.total.at[pl.ds(0, 16), c], self.sem.at[4, 1])
+        wait_bytes(self.pool.at[pl.ds(0, 16 + 15 + 3 + 15 + 16)], self.send)
+        wait_bytes(self.pool.at[pl.ds(0, 16)], self.got[4])
 
 
 def make_table(table, cells, counts):
@@ -519,48 +542,36 @@
     )
 
 
-def packed_copies(packed, bufs, send, recv):
-    a, b = coords()
-    copies = []
-    for i, (da, db) in enumerate(DIRS):
-        back = DIRS.index((-da, -db))
-        copies.append(
-            pltpu.make_async_remote_copy(
-                src_ref=packed, dst_ref=bufs.at[back], send_sem=send.at[i], recv_sem=recv.at[back],
-                device_id=(jnp.clip(a + da, 0, NA - 1), lax.rem(b + db + NB, NB)), device_id_type=MESH,
-            )
-        )
-    return copies
-
-
-def waits(copies):
-    for i, (da, db) in enumerate(DIRS):
-        when_exists(da, copies[i].wait_send)
-        when_exists(da, copies[DIRS.index((-da, -db))].wait_recv)
+def packed_start(packed, bufs, send, recv):
+    for da, db in DIRS:
+        pltpu.make_async_remote_copy(
+            src_ref=packed, dst_ref=bufs.at[DIRS.index((-da, -db))], send_sem=send, recv_sem=recv,
+            device_id=neighbour(da, db), device_id_type=MESH,
+        ).start()
 
 
 def kernel(
     values_hbm, cells_hbm, counts_hbm, embed_hbm, density_hbm, weight_hbm, cot_hbm,
     out_ref, total, back,
     values, cells, counts, embed, density, weight, cot,
-    table, tables, codes_mine, codes_got, recv, onehot, means, numbers, packed, packs,
+    table, tables, codes_mine, codes_got, recv, onehot, means, numbers, packed, packs, mean_strips, cot_strips,
     nN, nS, nW, nE, nNW, nNE, nSW, nSE,
     fN, fS, fW, fE, fNW, fNE, fSW, fSE,
     cN, cS, cW, cE, cNW, cNE, cSW, cSE,
-    x0, x1, g1, g0, slope0, cot_ext, up1, grid2, top, grads, picked,
+    x0, x1, g1, g0, slope0, cot_ext, up1, grid_out, top, grads, picked,
     *rest,
 ):
-    w1_bufs, w2_bufs, e_bufs = rest[0:5], rest[5:10], rest[10:15]
-    (load_sem, a2a_send, a2a_recv, back_send, back_recv, code_sem, halo_send, halo_recv, pack_send, pack_recv, cot_send, cot_recv,
-     w1_pair, w1_sem, w2_pair, w2_sem, e_sem) = rest[15:]
+    w1_bufs, w2_bufs, e_bufs = rest[0:6], rest[6:12], rest[12:18]
+    (pool, load_sem, a2a_send, a2a_recv, back_send, back_recv, code_sem, halo_sem, pack_sem, cot_sem,
+     w1_sem, w2_sem, e_sem) = rest[18:]
     a, _ = coords()
     pos = place()
     fbufs = (fN, fS, fW, fE, fNW, fNE, fSW, fSE)
     nbufs = (nN, nS, nW, nE, nNW, nNE, nSW, nSE)
     cbufs = (cN, cS, cW, cE, cNW, cNE, cSW, cSE)
-    w1 = Wave(0, pos, grads, total, w1_bufs, (w1_pair, w1_sem))
-    w2 = Wave(1, pos, grads, total, w2_bufs, (w2_pair, w2_sem))
-    es = EmbedSum(pos, grads, total, e_bufs, e_sem)
+    w1 = Wave(0, pos, grads, total, w1_bufs, w1_sem, pool)
+    w2 = Wave(1, pos, grads, total, w2_bufs, w2_sem, pool)
+    es = EmbedSum(pos, grads, total, e_bufs, e_sem, pool)
     barrier_signal()
     loads = [
         pltpu.make_async_copy(src, dst, load_sem.at[i])
@@ -573,22 +584,20 @@
     ]
     for load in loads:
         load.start()
-    halo_zero(fbufs)
-    halo_zero(cbufs)
-    halo_zero([packs.at[i] for i in range(8)])
     packed[...] = jnp.zeros_like(packed)
-    for load in loads[:3]:
+    for load in loads[:4]:
         load.wait()
+    make_pairs(cot, cot_strips)
     make_table(table, cells, counts)
     barrier_wait()
     codes_start(table, tables, code_sem)
-    exchange_start(values, recv, a2a_send, a2a_recv)
+    exchange_own(values, recv, a2a_recv)
+    exchange_start(values, recv, a2a_send, a2a_recv, FAR_Z)
     codes_forward(tables, codes_mine, codes_got, code_sem)
-    for load in loads[3:]:
+    for load in loads[4:]:
         load.wait()
     place_codes(codes_got, onehot, code_sem)
-    for lat in range(NA):
-        exchange_wait_recv(recv, a2a_recv, lat)
+    wait_bytes(recv, a2a_recv)
     both = jnp.concatenate([recv[...].reshape(SLOTS, F), jnp.ones((SLOTS, F), BF16)], axis=1)
     sums = lax.dot_general(
         onehot[...], both, (((0,), (0,)), ((), ())), preferred_element_type=F32
@@ -596,17 +605,17 @@
     numbers[...] = sums[:, F:]
     means[...] = (sums[:, :F] / jnp.maximum(sums[:, F:], 1.0)).astype(BF16).reshape(TR, TC, F)
     pack_numbers(numbers, packed)
-    halo = halo_copies(means, fbufs, HR, halo_send, halo_recv)
-    packs_out = packed_copies(packed, packs, pack_send, pack_recv)
-    halo_start(packs_out)
-    halo_start(halo)
-    cot_halo = halo_copies(cot, cbufs, HC, cot_send, cot_recv)
-    halo_start(cot_halo)
-    waits(packs_out)
+    make_strips(means, mean_strips)
+    packed_start(packed, packs, pack_sem.at[0], pack_sem.at[1])
+    halo_start(means, mean_strips, fbufs, HR, halo_sem.at[0], halo_sem.at[1])
+    pairs_start(cot, cot_strips, cbufs, cot_sem.at[0], cot_sem.at[1])
+    wait_bytes(packs, pack_sem.at[1])
+    halo_zero([packs.at[i] for i in range(8)])
     for i, (da, db) in enumerate(DIRS):
         first, count = PACKED[da]
         unpack_numbers(packs.at[i], first, count, nbufs[i])
-    waits(halo)
+    wait_bytes(pool.at[pl.ds(0, halo_units(HR, F))], halo_sem.at[1])
+    halo_zero(fbufs)
     for r in range(TR + 2 * HR):
         mean_row = ext_row(means, fbufs, HR, r).astype(BF16)
         logs = jnp.log(1.0 + numbers_row(numbers, nbufs, r))
@@ -627,22 +636,27 @@
         slope0[pl.ds(c * n, n)] = slope.reshape(n, W, CH)
         return carry
 
-    lax.fori_loop(0, 2, fwd0, 0)
-    waits(cot_halo)
+    lax.fori_loop(0, 2, fwd0, 0, unroll=True)
+    wait_bytes(pool.at[pl.ds(0, PAIR_UNITS)], cot_sem.at[1])
+    halo_zero(cbufs)
     for r in range(TR + 2 * HC):
-        cot_ext[r] = ext_row(cot, cbufs, HC, r)
+        cot_ext[r] = pairs_row(cot, cbufs, r)
     m = 10
 
     def fwd1(c, carry):
         pre = conv_fwd(x1, weight, 1, c * m, m)
         value, slope = gelu_parts(pre)
         old = x1[pl.ds(c * m + 1, m), :, CH : 2 * CH].reshape(m * W, CH).astype(F32)
-        grid2[pl.ds(c * m, m)] = (old + value).astype(BF16).reshape(m, W, CH)
+        final = (old + value).reshape(m, W, CH)
+        grid_out[8 * c : 8 * c + 8] = final[2 - 2 * c : 10 - 2 * c, SIDE : SIDE + TC].astype(BF16)
         grad = cot_ext[pl.ds(c * m, m)].reshape(m * W, CH) * slope
         put3(g1, pl.ds(c * m, m), grad.astype(BF16).astype(F32))
         return carry
 
-    lax.fori_loop(0, 2, fwd1, 0)
+    for c in range(2):
+        fwd1(c, 0)
+    field_copy = pltpu.make_async_copy(grid_out, out_ref, load_sem.at[7])
+    field_copy.start()
 
     grad1 = g1[2 : 2 + TR, SIDE : SIDE + TC, CH : 2 * CH].reshape(CELLS, CH)
     kernel_grad(x1, 2, grad1, grads, 288, (1, 2))
@@ -657,7 +671,7 @@
         put3(g0, pl.ds(c * k, k), grad.astype(BF16).astype(F32))
         return carry
 
-    lax.fori_loop(0, 2, bwd1, 0)
+    lax.fori_loop(0, 2, bwd1, 0, unroll=True)
     w1.rs1_start()
     kernel_grad(x1, 2, grad1, grads, 288, (0,))
     kernel_grad(x0, 3, g0[1 : 1 + TR, SIDE : SIDE + TC, CH : 2 * CH].reshape(CELLS, CH), grads, 0, (0, 1, 2))
@@ -669,7 +683,7 @@
         top[pl.ds(c * j, j)] = up.reshape(j, W, CH)[:, SIDE : SIDE + TC].astype(BF16)
         return carry
 
-    lax.fori_loop(0, 2, bwd0, 0)
+    lax.fori_loop(0, 2, bwd0, 0, unroll=True)
     w2.rs1_start()
     top_grad = top[...].reshape(CELLS, CH)
     mean_rows = means[...].reshape(CELLS, F)
@@ -684,11 +698,11 @@
     )
     scaled = (mean_grad / jnp.maximum(numbers[...], 1.0)).astype(BF16)
     picked[...] = jnp.dot(onehot[...], scaled, preferred_element_type=F32).astype(BF16).reshape(NT, CAP, F)
-    out_ref[...] = grid2[2 : 2 + TR, SIDE : SIDE + TC, :]
     w1.rs2_start()
     es.rs_start()
     w2.rs2_start()
-    exchange_start(picked, back, back_send, back_recv)
+    exchange_own(picked, back, back_recv)
+    exchange_start(picked, back, back_send, back_recv, FAR_Z)
     w1.ag2_start()
     es.sum_start()
     w2.ag2_start()
@@ -698,8 +712,11 @@
     w1.pair2_start()
     es.pair2_start()
     w2.pair2_start()
-    for lat in range(NA):
-        exchange_wait_recv(back, back_recv, lat)
+    field_copy.wait()
+    wait_bytes(packs, pack_sem.at[0])
+    wait_bytes(pool.at[pl.ds(0, halo_units(HR, F))], halo_sem.at[0])
+    wait_bytes(pool.at[pl.ds(0, PAIR_UNITS)], cot_sem.at[0])
+    wait_bytes(back, back_recv)
     exchange_wait_send(values, a2a_send)
     exchange_wait_send(picked, back_send)
     wait_bytes(tables.at[pl.ds(0, NB - 1)], code_sem.at[0])
@@ -740,7 +757,12 @@
 
 
 def halo_shapes(rows, width):
-    wide, side, corner = (rows, TC, width), (TR, STRIP, width), (rows, STRIP, width)
+    wide, side, corner = (rows, TC, width), (TR, SIDE, width), (rows, SIDE, width)
+    return [vmem(s) for s in (wide, wide, side, side, corner, corner, corner, corner)]
+
+
+def pair_shapes():
+    wide, side, corner = (HC, TC, CH), (TR // 4, 8, CH), (1, 8, CH)
     return [vmem(s) for s in (wide, wide, side, side, corner, corner, corner, corner)]
 
 
@@ -749,7 +771,7 @@
     units = 192 * per
     return [
         vmem((units, 8, 128)), vmem((units, 8, 128)), vmem((3, 3, 16 * per, 8, 128)),
-        vmem((3, 16 * per, 8, 128)), vmem((3, 15, per, 8, 128)),
+        vmem((3, 16 * per, 8, 128)), vmem((3, 15, per, 8, 128)), vmem((3, per, 8, 128)),
     ]
 
 
@@ -764,22 +786,23 @@
             jax.ShapeDtypeStruct((NT, CAP, F), BF16),
         ],
         in_specs=[ANY] * 7,
-        out_specs=[VM] * 3,
+        out_specs=[ANY] * 3,
         scratch_shapes=[
             vmem((NT, CAP, F)), vmem((CAP, NT), jnp.int32), vmem((1, NT), jnp.int32), vmem((F, CH)),
             vmem((1, CH), F32), vmem((2, 3, 3 * CH, CH)), vmem((TR, TC, CH)),
             vmem((2, CAP, NT)), vmem((NB, 2, CAP, NT)), vmem((NA, 1, NT), F32), vmem((NA, 1, NT), F32),
             vmem((NT, CAP, F)), vmem((SLOTS, CELLS)), vmem((TR, TC, F)), vmem((CELLS, F), F32),
-            vmem((8, 128), F32), vmem((8, 8, 128), F32),
+            vmem((8, 128), F32), vmem((8, 8, 128), F32), vmem((2, TR, SIDE, F)), vmem((2, TR // 4, 8, CH)),
             *[vmem((PACKED[da][1] * 128, 128), F32) for da, _ in DIRS],
-            *halo_shapes(HR, F), *halo_shapes(HC, CH),
+            *halo_shapes(HR, F), *pair_shapes(),
             vmem((24, W, 3 * CH)), vmem((22, W, 3 * CH)), vmem((20, W, 3 * CH)), vmem((18, W, 3 * CH)),
             vmem((22, W, CH), F32), vmem((20, W, CH), F32), vmem((18, W, CH), F32),
-            vmem((20, W, CH)), vmem((TR, TC, CH)), vmem((UNITS, 2, 8, 128)), vmem((NT, CAP, F)),
+            vmem((TR, TC, CH)), vmem((TR, TC, CH)), vmem((UNITS, 2, 8, 128)), vmem((NT, CAP, F)),
             *wave_shapes(0), *wave_shapes(1),
             vmem((16, 8, 128)), vmem((16, 8, 128)), vmem((15, 1, 8, 128)), vmem((1, 8, 128)), vmem((3, 1, 8, 128)),
-            DMA((7,)), DMA, DMA((NA,)), DMA, DMA((NA,)), DMA((4,)), DMA((8,)), DMA((8,)), DMA((8,)), DMA((8,)), DMA((8,)), DMA((8,)),
-            DMA((2,)), DMA((3, 5, 2)), DMA((2,)), DMA((3, 5, 2)), DMA((5, 2)),
+            vmem((1, 8, 128)),
+            vmem((POOL, 8, 128)), DMA((8,)), DMA, DMA, DMA, DMA, DMA((4,)), DMA((2,)), DMA((2,)), DMA((2,)),
+            DMA((15,)), DMA((15,)), DMA((6,)),
         ],
         compiler_params=pltpu.CompilerParams(
             collective_id=0, has_side_effects=True, vmem_limit_bytes=40 * 2**20

time: 71.2 us -> 68.6 us (0.963)
  Pallas kernels: 70.4 us -> 67.7 us
    pallas_call x1, Pallas kernels: 67.9 us -> 65.2 us  [body(): pl.pallas_call(kernel, out_shape=[jax.ShapeDtypeStruct((TR, TC, CH), BF16...]
where the time goes in v4:
time: 68.6 us; the launch traced here: 68.5 us
  Pallas kernels  67.7 us (99%)
  between operations  0.8 us (1%)
    pallas_call x1, Pallas kernels, body(): pl.pallas_call(kernel, out_shape=[jax.ShapeDtypeStruct((TR, TC, CH), BF16...  65.2 us
    pallas_call x1, Pallas kernels, body(): pl.pallas_call(write_kernel, out_shape=[jax.ShapeDtypeStruct((EMBED0 * 8,...  2.5 us

profile of v4, /device:TPU:1, one launch (start us, length us, event | category | flops | bytes accessed | tf_op | source)
XLA Modules:
  0.0 68.5 jit_solution(8548931220332999935)
XLA Ops:
  0.6 65.2 %shard_map.102 = (bf16[16,48,256]{2,1,0:T(8,128)(2,1)S(1)}, bf16[592,2,8,128]{3,2,1,0:T(8,128)(2,1)S(1)}, bf16[128,8,128]{2,1,0:T(8,128)(2,1)S(1)}) custom-call(bf16[128,8,128]{2,1,0:T(8,128)(2,1)} %bitcast.9, s32[8,128]{1,0:T(8,128)} %bitcast.10, s32[1,128]{1,0:T(1,128)} %counts_hbm.1, bf16[128,256]{1,0:T(8,128)(2,1)} %embed_hbm.1, f32[1,256]{1,0:T(1,128)} %bitcast.11, ...), custom_call_target="tpu_custom_call" | custom-call | tf_op jit(solution)/shard_map/pallas_call | solution.py:781
  65.8 2.5 %shard_map.103 = (f32[4608,256]{1,0:T(8,128)}, f32[128,256]{1,0:T(8,128)}, bf16[16,48,256]{2,1,0:T(8,128)(2,1)}, bf16[128,8,128]{2,1,0:T(8,128)(2,1)}) custom-call(bf16[592,2,8,128]{3,2,1,0:T(8,128)(2,1)S(1)} %get-tuple-element.11.total, bf16[16,48,256]{2,1,0:T(8,128)(2,1)S(1)} %get-tuple-element.12.field, bf16[128,8,128]{2,1,0:T(8,128)(2,1)S(1)} %get-tuple-element.13.back), custom_call_target="tpu_custom_call" | custom-call | tf_op jit(solution)/shard_map/pallas_call | solution.py:811

commit v5 on v4

--- a/solution.py
+++ b/solution.py
@@ -142,8 +142,11 @@
     return (lax.rem(a + da + NA, NA), lax.rem(b + db + NB, NB))
 
 
-def halo_start(src, strips, bufs, rows, send, recv):
-    for da, db in DIRS:
+SIDES, ENDS, REST = DIRS[2:4], DIRS[0:2], DIRS[0:2] + DIRS[4:]
+
+
+def halo_start(src, strips, bufs, rows, send, recv, dirs):
+    for da, db in dirs:
         back = DIRS.index((-da, -db))
         row = {-1: pl.ds(0, rows), 0: pl.ds(0, TR), 1: pl.ds(TR - rows, rows)}[da]
         whole = src if db == 0 else strips.at[(db + 1) // 2]
@@ -153,8 +156,23 @@
         ).start()
 
 
-def halo_units(rows, width):
-    return (2 * rows * TC + 2 * TR * SIDE + 4 * rows * SIDE) * width // 1024
+def corners_start(bufs, packs, sems, pack_sems):
+    for da, row in ((-1, 0), (1, TR - HR)):
+        peer = neighbour(da, 0)
+        for db, side in ((-1, 2), (1, 3)):
+            corner = DIRS.index((-da, db))
+            for src, dst, (send, recv) in (
+                (bufs[side].at[pl.ds(row, HR)], bufs[corner], sems),
+                (packs.at[side], packs.at[corner], pack_sems),
+            ):
+                pltpu.make_async_remote_copy(
+                    src_ref=src, dst_ref=dst, send_sem=send, recv_sem=recv,
+                    device_id=peer, device_id_type=MESH,
+                ).start()
+
+
+SIDE_UNITS = 2 * TR * SIDE * F // 1024
+REST_UNITS = (2 * HR * TC + 4 * HR * SIDE) * F // 1024
 
 
 def halo_zero(bufs):
@@ -193,17 +211,23 @@
         dst[rows, :, q * CH : (q + 1) * CH] = moved.astype(BF16).reshape(n, W, CH)
 
 
-def row_mask(first, n):
-    rows = lax.broadcasted_iota(jnp.int32, (n * W, CH), 0) // W + first
-    return (rows >= 0) & (rows < NA * TR)
+def zero_rows(dst, low, high):
+    a, _ = coords()
+    n = dst.shape[0]
+    for end, rows in ((0, slice(0, low)), (NA - 1, slice(n - high, n))):
+
+        def clear(rows=rows):
+            dst[rows] = jnp.zeros((rows.stop - rows.start,) + dst.shape[1:], dst.dtype)
+
+        pl.when(a == end)(clear)
 
 
 def gelu_parts(x):
     x2 = x * x
-    t = jnp.tanh(GC * x * (1.0 + GA * x2))
-    half = 0.5 * (1.0 + t)
+    t = jnp.tanh(x * (GC + (GC * GA) * x2))
+    half = 0.5 * t + 0.5
     value = x * half
-    slope = half + 0.5 * x * (1.0 - t * t) * (GC * (1.0 + 3.0 * GA * x2))
+    slope = half + value * (1.0 - half) * (2.0 * GC + (6.0 * GC * GA) * x2)
     return value, slope
 
 
@@ -292,13 +316,14 @@
     return total.astype(BF16)
 
 
+PLANE_STEPS = (
+    (2, 2), (2, 1), (2, 3), (1, 2), (3, 2), (1, 1), (1, 3), (3, 1), (3, 3), (2, 0), (0, 2), (1, 0), (3, 0), (0, 1), (0, 3),
+)
+
+
 def on_plane(pos, axes, fn):
-    def step(k, carry):
-        peer = along(along(pos, axes[0], k // 4), axes[1], lax.rem(k, 4))
-        fn(peer, k - 1)
-        return carry
-
-    lax.fori_loop(1, 16, step, 0)
+    for k, (da, db) in enumerate(PLANE_STEPS):
+        fn(along(along(pos, axes[0], da), axes[1], db), k)
 
 
 class Wave:
@@ -542,8 +567,8 @@
     )
 
 
-def packed_start(packed, bufs, send, recv):
-    for da, db in DIRS:
+def packed_start(packed, bufs, send, recv, dirs):
+    for da, db in dirs:
         pltpu.make_async_remote_copy(
             src_ref=packed, dst_ref=bufs.at[DIRS.index((-da, -db))], send_sem=send, recv_sem=recv,
             device_id=neighbour(da, db), device_id_type=MESH,
@@ -606,37 +631,49 @@
     means[...] = (sums[:, :F] / jnp.maximum(sums[:, F:], 1.0)).astype(BF16).reshape(TR, TC, F)
     pack_numbers(numbers, packed)
     make_strips(means, mean_strips)
-    packed_start(packed, packs, pack_sem.at[0], pack_sem.at[1])
-    halo_start(means, mean_strips, fbufs, HR, halo_sem.at[0], halo_sem.at[1])
-    pairs_start(cot, cot_strips, cbufs, cot_sem.at[0], cot_sem.at[1])
-    wait_bytes(packs, pack_sem.at[1])
-    halo_zero([packs.at[i] for i in range(8)])
-    for i, (da, db) in enumerate(DIRS):
-        first, count = PACKED[da]
-        unpack_numbers(packs.at[i], first, count, nbufs[i])
-    wait_bytes(pool.at[pl.ds(0, halo_units(HR, F))], halo_sem.at[1])
-    halo_zero(fbufs)
-    for r in range(TR + 2 * HR):
+    for i, dirs in enumerate((SIDES, ENDS)):
+        packed_start(packed, packs, pack_sem.at[0], pack_sem.at[1 + i], dirs)
+        halo_start(means, mean_strips, fbufs, HR, halo_sem.at[0], halo_sem.at[1 + i], dirs)
+
+    def unpack(dirs):
+        for da, db in dirs:
+            first, count = PACKED[da]
+            i = DIRS.index((da, db))
+            unpack_numbers(packs.at[i], first, count, nbufs[i])
+
+    def field_row(r):
         mean_row = ext_row(means, fbufs, HR, r).astype(BF16)
         logs = jnp.log(1.0 + numbers_row(numbers, nbufs, r))
         embedded = jnp.dot(mean_row, embed[...], preferred_element_type=F32) + jnp.concatenate(
             [logs, logs], axis=1
         ) * density[...]
-        put3(x0, slice(r, r + 1), embedded.astype(BF16).astype(F32))
-
-    n = 11
-
-    def fwd0(c, carry):
-        pre = conv_fwd(x0, weight, 0, c * n, n)
-        value, slope = gelu_parts(pre)
-        old = x0[pl.ds(c * n + 1, n), :, CH : 2 * CH].reshape(n * W, CH).astype(F32)
-        new = jnp.where(row_mask(a * TR - 3 + c * n, n), old + value, 0.0)
-        new = new.astype(BF16).astype(F32)
-        put3(x1, pl.ds(c * n, n), new)
-        slope0[pl.ds(c * n, n)] = slope.reshape(n, W, CH)
-        return carry
-
-    lax.fori_loop(0, 2, fwd0, 0, unroll=True)
+        put3(x0, slice(r, r + 1), embedded)
+
+    def fwd0(i, n):
+        value, slope = gelu_parts(conv_fwd(x0, weight, 0, i, n))
+        old = x0[i + 1 : i + 1 + n, :, CH : 2 * CH].reshape(n * W, CH).astype(F32)
+        put3(x1, slice(i, i + n), old + value)
+        slope0[i : i + n] = slope.reshape(n, W, CH)
+
+    wait_bytes(packs.at[pl.ds(0, 2)], pack_sem.at[1])
+    wait_bytes(pool.at[pl.ds(0, SIDE_UNITS)], halo_sem.at[1])
+    corners_start(fbufs, packs, (halo_sem.at[0], halo_sem.at[2]), (pack_sem.at[0], pack_sem.at[2]))
+    unpack(SIDES)
+    for r in range(HR, HR + TR):
+        field_row(r)
+    pairs_start(cot, cot_strips, cbufs, cot_sem.at[0], cot_sem.at[1])
+    fwd0(4, 7)
+    fwd0(11, 7)
+    wait_bytes(packs.at[pl.ds(0, 6)], pack_sem.at[2])
+    wait_bytes(pool.at[pl.ds(0, REST_UNITS)], halo_sem.at[2])
+    halo_zero([packs.at[i] for i in range(8)])
+    halo_zero(fbufs)
+    unpack(REST)
+    for r in tuple(range(HR)) + tuple(range(HR + TR, TR + 2 * HR)):
+        field_row(r)
+    fwd0(0, 4)
+    fwd0(18, 4)
+    zero_rows(x1, 3, 3)
     wait_bytes(pool.at[pl.ds(0, PAIR_UNITS)], cot_sem.at[1])
     halo_zero(cbufs)
     for r in range(TR + 2 * HC):
@@ -650,7 +687,7 @@
         final = (old + value).reshape(m, W, CH)
         grid_out[8 * c : 8 * c + 8] = final[2 - 2 * c : 10 - 2 * c, SIDE : SIDE + TC].astype(BF16)
         grad = cot_ext[pl.ds(c * m, m)].reshape(m * W, CH) * slope
-        put3(g1, pl.ds(c * m, m), grad.astype(BF16).astype(F32))
+        put3(g1, pl.ds(c * m, m), grad)
         return carry
 
     for c in range(2):
@@ -667,11 +704,11 @@
         up = conv_bwd(g1, weight, 1, c * k, k) + cot_ext[pl.ds(c * k + 1, k)].reshape(k * W, CH)
         up1[pl.ds(c * k, k)] = up.reshape(k, W, CH)
         grad = up * slope0[pl.ds(c * k + 2, k)].reshape(k * W, CH)
-        grad = jnp.where(row_mask(a * TR - 1 + c * k, k), grad, 0.0)
-        put3(g0, pl.ds(c * k, k), grad.astype(BF16).astype(F32))
+        put3(g0, pl.ds(c * k, k), grad)
         return carry
 
     lax.fori_loop(0, 2, bwd1, 0, unroll=True)
+    zero_rows(g0, 1, 1)
     w1.rs1_start()
     kernel_grad(x1, 2, grad1, grads, 288, (0,))
     kernel_grad(x0, 3, g0[1 : 1 + TR, SIDE : SIDE + TC, CH : 2 * CH].reshape(CELLS, CH), grads, 0, (0, 1, 2))
@@ -714,7 +751,7 @@
     w2.pair2_start()
     field_copy.wait()
     wait_bytes(packs, pack_sem.at[0])
-    wait_bytes(pool.at[pl.ds(0, halo_units(HR, F))], halo_sem.at[0])
+    wait_bytes(pool.at[pl.ds(0, SIDE_UNITS + REST_UNITS)], halo_sem.at[0])
     wait_bytes(pool.at[pl.ds(0, PAIR_UNITS)], cot_sem.at[0])
     wait_bytes(back, back_recv)
     exchange_wait_send(values, a2a_send)
@@ -801,7 +838,7 @@
             *wave_shapes(0), *wave_shapes(1),
             vmem((16, 8, 128)), vmem((16, 8, 128)), vmem((15, 1, 8, 128)), vmem((1, 8, 128)), vmem((3, 1, 8, 128)),
             vmem((1, 8, 128)),
-            vmem((POOL, 8, 128)), DMA((8,)), DMA, DMA, DMA, DMA, DMA((4,)), DMA((2,)), DMA((2,)), DMA((2,)),
+            vmem((POOL, 8, 128)), DMA((8,)), DMA, DMA, DMA, DMA, DMA((4,)), DMA((3,)), DMA((3,)), DMA((2,)),
             DMA((15,)), DMA((15,)), DMA((6,)),
         ],
         compiler_params=pltpu.CompilerParams(

time: 68.6 us -> 67.2 us (0.980)
  Pallas kernels: 67.7 us -> 66.3 us
    pallas_call x1, Pallas kernels: 65.2 us -> 63.8 us  [body(): pl.pallas_call(kernel, out_shape=[jax.ShapeDtypeStruct((TR, TC, CH), BF16...]
where the time goes in v5:
time: 67.2 us; the launch traced here: 67.1 us
  Pallas kernels  66.3 us (99%)
  between operations  0.8 us (1%)
    pallas_call x1, Pallas kernels, body(): pl.pallas_call(kernel, out_shape=[jax.ShapeDtypeStruct((TR, TC, CH), BF16...  63.8 us
    pallas_call x1, Pallas kernels, body(): pl.pallas_call(write_kernel, out_shape=[jax.ShapeDtypeStruct((EMBED0 * 8,...  2.5 us

profile of v5, /device:TPU:1, one launch (start us, length us, event | category | flops | bytes accessed | tf_op | source)
XLA Modules:
  0.0 67.1 jit_solution(15670826211052679397)
XLA Ops:
  0.6 63.8 %shard_map.102 = (bf16[16,48,256]{2,1,0:T(8,128)(2,1)S(1)}, bf16[592,2,8,128]{3,2,1,0:T(8,128)(2,1)S(1)}, bf16[128,8,128]{2,1,0:T(8,128)(2,1)S(1)}) custom-call(bf16[128,8,128]{2,1,0:T(8,128)(2,1)} %bitcast.9, s32[8,128]{1,0:T(8,128)} %bitcast.10, s32[1,128]{1,0:T(1,128)} %counts_hbm.1, bf16[128,256]{1,0:T(8,128)(2,1)} %embed_hbm.1, f32[1,256]{1,0:T(1,128)} %bitcast.11, ...), custom_call_target="tpu_custom_call" | custom-call | tf_op jit(solution)/shard_map/pallas_call | solution.py:818
  64.4 2.5 %shard_map.103 = (f32[4608,256]{1,0:T(8,128)}, f32[128,256]{1,0:T(8,128)}, bf16[16,48,256]{2,1,0:T(8,128)(2,1)}, bf16[128,8,128]{2,1,0:T(8,128)(2,1)}) custom-call(bf16[592,2,8,128]{3,2,1,0:T(8,128)(2,1)S(1)} %get-tuple-element.11.total, bf16[16,48,256]{2,1,0:T(8,128)(2,1)S(1)} %get-tuple-element.12.field, bf16[128,8,128]{2,1,0:T(8,128)(2,1)S(1)} %get-tuple-element.13.back), custom_call_target="tpu_custom_call" | custom-call | tf_op jit(solution)/shard_map/pallas_call | solution.py:848

commit v6 on v5

--- a/solution.py
+++ b/solution.py
@@ -658,10 +658,10 @@
     wait_bytes(packs.at[pl.ds(0, 2)], pack_sem.at[1])
     wait_bytes(pool.at[pl.ds(0, SIDE_UNITS)], halo_sem.at[1])
     corners_start(fbufs, packs, (halo_sem.at[0], halo_sem.at[2]), (pack_sem.at[0], pack_sem.at[2]))
+    pairs_start(cot, cot_strips, cbufs, cot_sem.at[0], cot_sem.at[1])
     unpack(SIDES)
     for r in range(HR, HR + TR):
         field_row(r)
-    pairs_start(cot, cot_strips, cbufs, cot_sem.at[0], cot_sem.at[1])
     fwd0(4, 7)
     fwd0(11, 7)
     wait_bytes(packs.at[pl.ds(0, 6)], pack_sem.at[2])

time: 67.2 us -> 67 us (level)
  no operation moved by 1% of the time
where the time goes in v6:
time: 67 us; the launch traced here: 66.9 us
  Pallas kernels  66.1 us (99%)
  between operations  0.8 us (1%)
    pallas_call x1, Pallas kernels, body(): pl.pallas_call(kernel, out_shape=[jax.ShapeDtypeStruct((TR, TC, CH), BF16...  63.6 us
    pallas_call x1, Pallas kernels, body(): pl.pallas_call(write_kernel, out_shape=[jax.ShapeDtypeStruct((EMBED0 * 8,...  2.5 us

profile of v6, /device:TPU:1, one launch (start us, length us, event | category | flops | bytes accessed | tf_op | source)
XLA Modules:
  0.0 66.9 jit_solution(15758757409883998721)
XLA Ops:
  0.6 63.6 %shard_map.102 = (bf16[16,48,256]{2,1,0:T(8,128)(2,1)S(1)}, bf16[592,2,8,128]{3,2,1,0:T(8,128)(2,1)S(1)}, bf16[128,8,128]{2,1,0:T(8,128)(2,1)S(1)}) custom-call(bf16[128,8,128]{2,1,0:T(8,128)(2,1)} %bitcast.9, s32[8,128]{1,0:T(8,128)} %bitcast.10, s32[1,128]{1,0:T(1,128)} %counts_hbm.1, bf16[128,256]{1,0:T(8,128)(2,1)} %embed_hbm.1, f32[1,256]{1,0:T(1,128)} %bitcast.11, ...), custom_call_target="tpu_custom_call" | custom-call | tf_op jit(solution)/shard_map/pallas_call | solution.py:818
  64.2 2.5 %shard_map.103 = (f32[4608,256]{1,0:T(8,128)}, f32[128,256]{1,0:T(8,128)}, bf16[16,48,256]{2,1,0:T(8,128)(2,1)}, bf16[128,8,128]{2,1,0:T(8,128)(2,1)}) custom-call(bf16[592,2,8,128]{3,2,1,0:T(8,128)(2,1)S(1)} %get-tuple-element.11.total, bf16[16,48,256]{2,1,0:T(8,128)(2,1)S(1)} %get-tuple-element.12.field, bf16[128,8,128]{2,1,0:T(8,128)(2,1)S(1)} %get-tuple-element.13.back), custom_call_target="tpu_custom_call" | custom-call | tf_op jit(solution)/shard_map/pallas_call | solution.py:848
